TPU v7x, 128 devices: a whole 4x4x4 slice. The times are simulated.
128 devices in a mesh: wall: 8 (over z, core), depth: 16 (over y, x).
Axes of the slice: x: 4, y: 4, z: 4, core: 2. Of those that a mesh axis runs over, the one named last changes fastest.
Arguments:
- pressure: float32 [8, 256, 1024], P(None, 'depth', 'wall'), may hold values from 0.5 to 2
- layer: int32 [8, 256, 1024], P(None, 'depth', 'wall'), may hold values from 0 to 7
- permeability: float32 [2, 8], replicated, may hold values from 1 to 3
- loading: float32 [8, 256, 1024], P(None, 'depth', 'wall'), may hold values from -6 to 6
- spring: float32 [1024], P('wall'), may hold values from -4 to 4
- contact: int32 [64], P('wall'), may hold values 0 or 1
Outputs:
- pressure_out: float32 [8, 256, 1024], P(None, 'depth', 'wall')
- spring_out: float32 [1024], P('wall')
All inputs are finite; a program needn't handle non-finite values. No bound on the sum of `contact` on one device may be relied on, other than what follows from the above.
Results may differ from a plain program's by a relative error of at most 0.0017.
Values sent between devices are 32-bit elements; how exact they have to be, the bound alone decides.
A program may use at most 64 MiB of HBM per device.

v0:
```python
import jax
import jax.numpy as jnp
from jax import lax
from jax.sharding import PartitionSpec as P

LAYERS = 8
BLOCK = 16
SUBSTEPS = 3
OUTER = 2
VNUM = 512


ALONG_RATE = 0.1
ACROSS_RATE = 0.06
WALL_GAIN = 1.0
SOURCE_RATE = 1.0
SPRING_KEEP = 0.5
SPRING_DRIVE = 2.0


def entering(shard, axis, combine, identity, reverse):
    length, mine = (lax.axis_size(axis), lax.axis_index(axis))
    everything = lax.all_gather(shard, axis)
    start = jnp.broadcast_to(jnp.asarray(identity, shard.dtype), shard.shape)

    def step(k, before):
        at = length - 1 - k if reverse else k
        reached = at > mine if reverse else at < mine
        new = combine(before, everything[at])
        return jnp.where(reached, new, before)

    return lax.fori_loop(0, length, step, start)


def with_halo(cells, sides, width):
    for axis, dim in sides:
        count = lax.axis_size(axis)
        ends = count - 1
        head = lax.slice_in_dim(cells, 0, width, axis=dim)
        tail = lax.slice_in_dim(cells, cells.shape[dim] - width, cells.shape[dim], axis=dim)
        cells = jnp.concatenate(
            [
                lax.ppermute(tail, axis, [(i, (i + 1) % count) for i in range(ends)]),
                cells,
                lax.ppermute(head, axis, [((i + 1) % count, i) for i in range(ends)]),
            ],
            axis=dim,
        )
    return cells


def lookup(layer, table_row):
    totals = jnp.zeros(layer.shape, jnp.float32)
    for soil_level in range(LAYERS):
        totals = totals + jnp.where(layer == soil_level, table_row[soil_level], jnp.float32(0.0))
    return totals


def harmonic(upper_perm, lower_perm):
    return 2.0 * upper_perm * lower_perm / (upper_perm + lower_perm)


def horizontal(field, leftward, rightward, lateral_perm, wall_value, contact_share):
    along = ALONG_RATE * lateral_perm * (leftward + rightward - 2.0 * field)
    change = field[1:] - field[:-1]
    blank = jnp.zeros_like(field[:1])
    across = jnp.concatenate([change, blank], 0) - jnp.concatenate([blank, change], 0)
    wall_flux = contact_share[None, :] * (wall_value[None, :] - field[0])
    wall_term = jnp.concatenate([wall_flux[None], jnp.zeros_like(field[1:])], 0)
    return along + ACROSS_RATE * lateral_perm * (across + wall_term)


def compose(latter, earlier):
    entries = []
    for matrix_row in range(3):
        for column in range(3):
            entries.append(
                latter[3 * matrix_row] * earlier[column]
                + latter[3 * matrix_row + 1] * earlier[3 + column]
                + latter[3 * matrix_row + 2] * earlier[6 + column]
            )
    stacked = jnp.stack(entries)
    largest = jnp.max(jnp.abs(stacked), axis=0)
    return stacked / largest


def forward_join(earlier, latter):
    return compose(latter, earlier)


def backward_join(earlier, latter):
    return jnp.stack([latter[0] * earlier[0], latter[1] + latter[0] * earlier[1]])


def forward_maps(upward, downward, diagonal, right_side):
    blank = jnp.zeros_like(right_side)
    matrices = jnp.stack(
        [blank, blank, -downward, blank, upward, right_side, upward, blank, diagonal]
    )
    prefix = lax.associative_scan(forward_join, matrices, axis=2)
    totals = prefix[:, :, -1, :]
    unit_plane = jnp.ones_like(totals[0])
    empty_plane = jnp.zeros_like(totals[0])
    identity = jnp.stack([unit_plane if entry in (0, 4, 8) else empty_plane for entry in range(9)])
    incoming = entering(totals, "depth", forward_join, identity, False)
    state_in = [incoming[2][:, None, :], incoming[5][:, None, :], incoming[8][:, None, :]]
    numer_slope = prefix[0] * state_in[0] + prefix[1] * state_in[1] + prefix[2] * state_in[2]
    numer_offset = prefix[3] * state_in[0] + prefix[4] * state_in[1] + prefix[5] * state_in[2]
    pivot_value = prefix[6] * state_in[0] + prefix[7] * state_in[1] + prefix[8] * state_in[2]
    return (numer_slope / pivot_value, numer_offset / pivot_value)


def back_solve(slopes, offsets):
    affine_maps = jnp.stack([-slopes, offsets])
    suffix = lax.associative_scan(backward_join, affine_maps, reverse=True, axis=2)
    device_maps = suffix[:, :, 0, :]
    unit_plane = jnp.ones_like(device_maps[0])
    empty_plane = jnp.zeros_like(device_maps[0])
    map_identity = jnp.stack([unit_plane, empty_plane])
    beneath = entering(device_maps, "depth", backward_join, map_identity, True)
    return suffix[1] + suffix[0] * beneath[1][:, None, :]


def line_solve(upward, downward, diagonal, right_side):
    slopes, offsets = forward_maps(upward, downward, diagonal, right_side)
    return back_solve(slopes, offsets)


def on_device(pressure, layer, permeability, loading, spring, contact):
    device_index = lax.axis_index("depth")
    depth_count = lax.axis_size("depth")
    rows_here = pressure.shape[1]
    vertical_perm = lookup(layer, permeability[0])
    lateral_perm = lookup(layer, permeability[1])
    widened = with_halo(vertical_perm, (("depth", 1),), 1)
    upward = VNUM * harmonic(widened[:, :-2], widened[:, 1:-1])
    downward = VNUM * harmonic(widened[:, 1:-1], widened[:, 2:])
    row_number = lax.broadcasted_iota(jnp.int32, (1, rows_here, 1), 1)
    first_row = (row_number == 0) & (device_index == 0)
    upward = jnp.where(first_row, VNUM * vertical_perm, upward)
    diagonal = 1.0 + upward + downward
    contact_share = jnp.repeat(contact.astype(jnp.float32), BLOCK)
    depth_rows = (
        device_index * rows_here + lax.broadcasted_iota(jnp.int32, (rows_here,), 0)
    ).astype(jnp.float32)
    total_rows = rows_here * depth_count
    weights = (depth_rows + 0.5) / total_rows
    field = pressure
    for outer_step in range(OUTER):
        wall_value = WALL_GAIN * spring
        for substep in range(SUBSTEPS):
            padded = with_halo(field, (("wall", 2),), 1)
            right_side = (
                field
                + horizontal(
                    field,
                    padded[..., :-2],
                    padded[..., 2:],
                    lateral_perm,
                    wall_value,
                    contact_share,
                )
                + SOURCE_RATE * loading
            )
            field = line_solve(upward, downward, diagonal, right_side)
        partial_moment = jnp.sum(weights[:, None] * field[0], axis=0) / total_rows
        moment = lax.psum(partial_moment, "depth")
        spring = SPRING_KEEP * spring + SPRING_DRIVE * contact_share * moment
    return (field, spring)


def solution(mesh):
    placed = (
        P(None, "depth", "wall"),
        P(None, "depth", "wall"),
        P(),
        P(None, "depth", "wall"),
        P("wall"),
        P("wall"),
    )
    return jax.shard_map(
        on_device,
        mesh=mesh,
        in_specs=placed,
        out_specs=(P(None, "depth", "wall"), P("wall")),
        check_vma=False,
    )
```

profile of v0, /device:TPU:96, one launch (start us, length us, event | category | flops | bytes accessed | tf_op | source)
XLA Modules:
  0.0 543.1 jit_solution(2212716996207832194)
XLA Ops:
  0.6 2.0 fusion.269
  2.6 5.9 %select_add_fusion = (f32[8,16,128]{2,1,0:T(8,128)S(1)}, pred[8,16,128]{2,1,0:T(8,128)(4,1)S(1)}, pred[8,16,128]{2,1,0:T(8,128)(4,1)S(1)}, pred[8,16,128]{2,1,0:...) fusion(f32[]{:T(128)} %bitcast.83, f32[]{:T(128)} %bitcast.82, ...), kind=kLoop, calls=%fused_computation.1003 | loop fusion | flops 376832 | bytes 262176 | tf_op jit(solution)/shard_map/add | solution.py:55
  8.5 5.0 select_add_fusion.1
  13.5 1.3 collective-permute-start
  14.8 4.5 collective-permute-start.1
  19.5 1.9 collective-permute-start.2
  21.4 3.6 collective-permute-start.3
  29.9 0.7 copy-done.7
  31.6 0.9 copy-done.25
  37.7 1.0 pad.320
  38.6 1.0 pad.321
  42.4 0.7 copy-done.28
  44.8 26.8 %all-gather = f32[144,8,1,128]{3,1,2,0:T(8,128)S(1)} all-gather(f32[9,8,1,128]{3,1,2,0:T(8,128)S(1)} %slice_add_fusion.17), channel_id=2, replica_groups=mesh['wall'=8,'depth'=16] {'depth'}, dimensions={0}, use_global_device_ids=true | all-gather | bytes 626688 | tf_op jit(solution)/shard_map/all_gather | solution.py:23
  71.6 4.4 while.168
  77.3 21.5 %all-gather.1 = f32[32,8,1,128]{3,1,2,0:T(8,128)S(1)} all-gather(f32[2,8,1,128]{3,1,2,0:T(8,128)S(1)} %slice.14893), channel_id=3, replica_groups=mesh['wall'=8,'depth'=16] {'depth'}, dimensions={0}, use_global_device_ids=true | all-gather | bytes 139264 | tf_op jit(solution)/shard_map/all_gather | solution.py:23
  98.7 0.9 while.169
  100.5 2.0 collective-permute-start.4
  102.6 3.6 collective-permute-start.5
  106.9 1.2 collective-permute-done.5
  113.8 1.0 pad.336
  114.7 1.0 pad.337
  116.7 0.7 slice-done.1
  120.7 23.5 %all-gather.2 = f32[144,8,1,128]{3,1,2,0:T(8,128)S(1)} all-gather(f32[9,8,1,128]{3,1,2,0:T(8,128)S(1)} %bitcast.1184), channel_id=4, replica_groups=mesh['wall'=8,'depth'=16] {'depth'}, dimensions={0}, use_global_device_ids=true | all-gather | bytes 626688 | tf_op jit(solution)/shard_map/all_gather | solution.py:23
  144.1 4.3 while.170
  151.1 21.7 %all-gather.3 = f32[32,8,1,128]{3,1,2,0:T(8,128)S(1)} all-gather(f32[2,8,1,128]{3,1,2,0:T(8,128)S(1)} %bitcast.1201), channel_id=5, replica_groups=mesh['wall'=8,'depth'=16] {'depth'}, dimensions={0}, use_global_device_ids=true | all-gather | bytes 139264 | tf_op jit(solution)/shard_map/all_gather | solution.py:23
  172.8 0.9 while.171
  174.7 1.9 collective-permute-start.6
  176.6 3.6 collective-permute-start.7
  180.9 1.2 collective-permute-done.7
  187.7 1.0 pad.352
  188.7 1.0 pad.353
  194.6 23.4 %all-gather.4 = f32[144,8,1,128]{3,1,2,0:T(8,128)S(1)} all-gather(f32[9,8,1,128]{3,1,2,0:T(8,128)S(1)} %bitcast.1185), channel_id=6, replica_groups=mesh['wall'=8,'depth'=16] {'depth'}, dimensions={0}, use_global_device_ids=true | all-gather | bytes 626688 | tf_op jit(solution)/shard_map/all_gather | solution.py:23
  218.0 4.3 while.172
  225.0 21.6 %all-gather.5 = f32[32,8,1,128]{3,1,2,0:T(8,128)S(1)} all-gather(f32[2,8,1,128]{3,1,2,0:T(8,128)S(1)} %bitcast.1202), channel_id=7, replica_groups=mesh['wall'=8,'depth'=16] {'depth'}, dimensions={0}, use_global_device_ids=true | all-gather | bytes 139264 | tf_op jit(solution)/shard_map/all_gather | solution.py:23
  246.6 0.9 while.173
  247.8 38.2 %psum.14 = f32[128]{0:T(128)S(1)} all-reduce(f32[128]{0:T(128)S(1)} %broadcast_multiply_fusion.1), channel_id=1, replica_groups=mesh['wall'=8,'depth'=16] {'depth'}, use_global_device_ids=true, to_apply=%region_37.38 | all-reduce | flops 128 | bytes 1024 | tf_op jit(solution)/shard_map/psum | solution.py:167
  286.7 1.9 collective-permute-start.8
  288.6 3.6 collective-permute-start.9
  292.3 1.9 collective-permute-done.9
  299.2 1.0 pad.368
  300.2 1.0 pad.369
  306.1 21.1 %all-gather.6 = f32[144,8,1,128]{3,1,2,0:T(8,128)S(1)} all-gather(f32[9,8,1,128]{3,1,2,0:T(8,128)S(1)} %bitcast.1186), channel_id=8, replica_groups=mesh['wall'=8,'depth'=16] {'depth'}, dimensions={0}, use_global_device_ids=true | all-gather | bytes 626688 | tf_op jit(solution)/shard_map/all_gather | solution.py:23
  327.2 4.3 while.174
  334.2 24.1 %all-gather.7 = f32[32,8,1,128]{3,1,2,0:T(8,128)S(1)} all-gather(f32[2,8,1,128]{3,1,2,0:T(8,128)S(1)} %bitcast.1203), channel_id=9, replica_groups=mesh['wall'=8,'depth'=16] {'depth'}, dimensions={0}, use_global_device_ids=true | all-gather | bytes 139264 | tf_op jit(solution)/shard_map/all_gather | solution.py:23
  358.3 0.9 while.175
  360.1 1.9 collective-permute-start.10
  362.0 3.6 collective-permute-start.11
  365.7 1.9 collective-permute-done.11
  372.6 1.0 pad.384
  373.6 1.0 pad.385
  379.5 21.1 %all-gather.8 = f32[144,8,1,128]{3,1,2,0:T(8,128)S(1)} all-gather(f32[9,8,1,128]{3,1,2,0:T(8,128)S(1)} %bitcast.1187), channel_id=10, replica_groups=mesh['wall'=8,'depth'=16] {'depth'}, dimensions={0}, use_global_device_ids=true | all-gather | bytes 626688 | tf_op jit(solution)/shard_map/all_gather | solution.py:23
  400.6 4.3 while.176
  407.6 23.9 %all-gather.9 = f32[32,8,1,128]{3,1,2,0:T(8,128)S(1)} all-gather(f32[2,8,1,128]{3,1,2,0:T(8,128)S(1)} %bitcast.1204), channel_id=11, replica_groups=mesh['wall'=8,'depth'=16] {'depth'}, dimensions={0}, use_global_device_ids=true | all-gather | bytes 139264 | tf_op jit(solution)/shard_map/all_gather | solution.py:23
  431.5 0.9 while.177
  432.7 1.9 collective-permute-start.12
  434.6 3.6 collective-permute-start.13
  438.3 1.8 collective-permute-done.13
  444.6 1.0 pad.400
  445.6 1.0 pad.401
  450.8 21.1 %all-gather.10 = f32[144,8,1,128]{3,1,2,0:T(8,128)S(1)} all-gather(f32[9,8,1,128]{3,1,2,0:T(8,128)S(1)} %bitcast.1188), channel_id=12, replica_groups=mesh['wall'=8,'depth'=16] {'depth'}, dimensions={0}, use_global_device_ids=true | all-gather | bytes 626688 | tf_op jit(solution)/shard_map/all_gather | solution.py:23
  471.9 4.3 while.178
  478.9 23.9 %all-gather.11 = f32[32,8,1,128]{3,1,2,0:T(8,128)S(1)} all-gather(f32[2,8,1,128]{3,1,2,0:T(8,128)S(1)} %bitcast.1205), channel_id=13, replica_groups=mesh['wall'=8,'depth'=16] {'depth'}, dimensions={0}, use_global_device_ids=true | all-gather | bytes 139264 | tf_op jit(solution)/shard_map/all_gather | solution.py:23
  502.8 0.9 while.179
  504.4 38.1 %psum.15 = f32[128]{0:T(128)S(1)} all-reduce(f32[128]{0:T(128)S(1)} %broadcast_multiply_fusion), channel_id=1, replica_groups=mesh['wall'=8,'depth'=16] {'depth'}, use_global_device_ids=true, to_apply=%region_75.76 | all-reduce | flops 128 | bytes 1024 | tf_op jit(solution)/shard_map/psum | solution.py:167
  (2356 shorter events, 98.9 us)
Async XLA Ops:
  8.5 10.9 %copy-start.27 = (f32[8,16,128]{2,1,0:T(8,128)S(1)}, f32[8,16,128]{2,1,0:T(8,128)}, u32[]{:S(2)}) copy-start(f32[8,16,128]{2,1,0:T(8,128)} %param.30) | copy-start | bytes 196612
  13.5 16.2 %collective-permute-start = (f32[8,1,128]{2,1,0:T(1,128)S(1)}, f32[8,1,128]{2,1,0:T(1,128)S(1)}, u32[]{:S(2)}, u32[]{:S(2)}) collective-permute-start(f32[8,1,128]{2,1,0:T(1,128)S(1)} %get-tuple-element.1406), channel_id=1, source_target_pairs={{1,0},{2,1},{3,2},{4,3},{5,4},{6,5},{7,6},{8,7},{9,8},{10,9},{11,1... | collective-permute-start | bytes 12296 | tf_op jit(solution)/shard_map/ppermute | solution.py:45
  14.8 15.0 %collective-permute-start.1 = (f32[8,1,128]{2,1,0:T(1,128)S(1)}, f32[8,1,128]{2,1,0:T(1,128)S(1)}, u32[]{:S(2)}, u32[]{:S(2)}) collective-permute-start(f32[8,1,128]{2,1,0:T(1,128)S(1)} %get-tuple-element.1405), channel_id=1, source_target_pairs={{0,1},{1,2},{2,3},{3,4},{4,5},{5,6},{6,7},{7,8},{8,9},{9,10},{10,1... | collective-permute-start | bytes 12296 | tf_op jit(solution)/shard_map/ppermute | solution.py:43
  19.5 10.4 %collective-permute-start.2 = (f32[8,16,1]{2,1,0:T(8,128)S(1)}, f32[8,16,1]{2,1,0:T(8,128)S(1)}, u32[]{:S(2)}, u32[]{:S(2)}) collective-permute-start(f32[8,16,1]{2,1,0:T(8,128)S(1)} %get-tuple-element.1403), channel_id=1, source_target_pairs={{0,16},{16,32},{32,48},{48,64},{64,80},{80,96},{96,112},{1,17},{17... | collective-permute-start | bytes 1544 | tf_op jit(solution)/shard_map/ppermute | solution.py:43
  21.4 8.5 %collective-permute-start.3 = (f32[8,16,1]{2,1,0:T(8,128)S(1)}, f32[8,16,1]{2,1,0:T(8,128)S(1)}, u32[]{:S(2)}, u32[]{:S(2)}) collective-permute-start(f32[8,16,1]{2,1,0:T(8,128)S(1)} %get-tuple-element.1404), channel_id=1, source_target_pairs={{16,0},{32,16},{48,32},{64,48},{80,64},{96,80},{112,96},{17,1},{33... | collective-permute-start | bytes 1544 | tf_op jit(solution)/shard_map/ppermute | solution.py:45
  26.4 0.7 copy-start.51
  26.5 1.4 copy-start.44
  27.1 1.3 copy-start.40
  28.4 0.7 copy-start
  28.4 0.7 copy-start.48
  29.8 0.8 copy-start.7
  31.5 0.9 copy-start.25
  32.4 0.8 copy-start.23
  33.5 2.6 copy-start.15
  35.2 1.1 copy-start.24
  40.6 0.8 slice-start
  42.4 0.8 copy-start.28
  44.8 26.8 %copy-start.2 = (f32[9,8,128]{2,1,0:T(8,128)S(1)}, f32[9,8,128]{2,1,0:T(8,128)}, u32[]{:S(2)}) copy-start(f32[9,8,128]{2,1,0:T(8,128)} %copy-done) | copy-start | bytes 110596
  77.2 21.5 %copy-start.10 = (f32[2,8,128]{2,1,0:T(8,128)S(1)}, f32[2,8,128]{2,1,0:T(8,128)}, u32[]{:S(2)}) copy-start(f32[2,8,128]{2,1,0:T(8,128)} %copy-done.8) | copy-start | bytes 24580
  100.4 7.9 %copy-start.26 = (f32[9,8,16,128]{3,2,1,0:T(8,128)S(1)}, f32[9,8,16,128]{3,2,1,0:T(8,128)}, u32[]{:S(2)}) copy-start(f32[9,8,16,128]{3,2,1,0:T(8,128)} %copy-done.25) | copy-start | bytes 1769476
  100.5 6.3 %collective-permute-start.4 = (f32[8,16,1]{2,1,0:T(8,128)S(1)}, f32[8,16,1]{2,1,0:T(8,128)S(1)}, u32[]{:S(2)}, u32[]{:S(2)}) collective-permute-start(f32[8,16,1]{2,1,0:T(8,128)S(1)} %get-tuple-element.1391), channel_id=1, source_target_pairs={{0,16},{16,32},{32,48},{48,64},{64,80},{80,96},{96,112},{1,17},{17... | collective-permute-start | bytes 1544 | tf_op jit(solution)/shard_map/ppermute | solution.py:43
  102.6 5.5 %collective-permute-start.5 = (f32[8,16,1]{2,1,0:T(8,128)S(1)}, f32[8,16,1]{2,1,0:T(8,128)S(1)}, u32[]{:S(2)}, u32[]{:S(2)}) collective-permute-start(f32[8,16,1]{2,1,0:T(8,128)S(1)} %get-tuple-element.1392), channel_id=1, source_target_pairs={{16,0},{32,16},{48,32},{64,48},{80,64},{96,80},{112,96},{17,1},{33... | collective-permute-start | bytes 1544 | tf_op jit(solution)/shard_map/ppermute | solution.py:45
  109.8 2.6 copy-start.16
  116.7 0.8 slice-start.1
  118.5 0.8 copy-start.29
  120.6 23.5 %copy-start.3 = (f32[9,8,128]{2,1,0:T(8,128)S(1)}, f32[9,8,128]{2,1,0:T(8,128)}, u32[]{:S(2)}) copy-start(f32[9,8,128]{2,1,0:T(8,128)} %copy-done) | copy-start | bytes 110596
  151.1 21.7 %copy-start.11 = (f32[2,8,128]{2,1,0:T(8,128)S(1)}, f32[2,8,128]{2,1,0:T(8,128)}, u32[]{:S(2)}) copy-start(f32[2,8,128]{2,1,0:T(8,128)} %copy-done.8) | copy-start | bytes 24580
  173.8 8.4 %copy-start.22 = (f32[9,8,16,128]{3,2,1,0:T(8,128)S(1)}, f32[9,8,16,128]{3,2,1,0:T(8,128)}, u32[]{:S(2)}) copy-start(f32[9,8,16,128]{3,2,1,0:T(8,128)} %get-tuple-element.1334) | copy-start | bytes 1769476
  174.0 0.7 copy-start.36
  174.0 0.7 copy-start.46
  174.7 6.2 %collective-permute-start.6 = (f32[8,16,1]{2,0,1:T(8,128)S(1)}, f32[8,16,1]{2,0,1:T(8,128)S(1)}, u32[]{:S(2)}, u32[]{:S(2)}) collective-permute-start(f32[8,16,1]{2,0,1:T(8,128)S(1)} %get-tuple-element.1381), channel_id=1, source_target_pairs={{0,16},{16,32},{32,48},{48,64},{64,80},{80,96},{96,112},{1,17},{17... | collective-permute-start | bytes 1544 | tf_op jit(solution)/shard_map/ppermute | solution.py:43
  176.6 5.5 %collective-permute-start.7 = (f32[8,16,1]{2,0,1:T(8,128)S(1)}, f32[8,16,1]{2,0,1:T(8,128)S(1)}, u32[]{:S(2)}, u32[]{:S(2)}) collective-permute-start(f32[8,16,1]{2,0,1:T(8,128)S(1)} %get-tuple-element.1382), channel_id=1, source_target_pairs={{16,0},{32,16},{48,32},{64,48},{80,64},{96,80},{112,96},{17,1},{33... | collective-permute-start | bytes 1544 | tf_op jit(solution)/shard_map/ppermute | solution.py:45
  183.7 2.6 copy-start.17
  190.6 0.8 slice-start.2
  192.5 0.8 copy-start.30
  194.6 23.4 %copy-start.4 = (f32[9,8,128]{2,1,0:T(8,128)S(1)}, f32[9,8,128]{2,1,0:T(8,128)}, u32[]{:S(2)}) copy-start(f32[9,8,128]{2,1,0:T(8,128)} %copy-done) | copy-start | bytes 110596
  225.0 21.6 %copy-start.12 = (f32[2,8,128]{2,1,0:T(8,128)S(1)}, f32[2,8,128]{2,1,0:T(8,128)}, u32[]{:S(2)}) copy-start(f32[2,8,128]{2,1,0:T(8,128)} %copy-done.8) | copy-start | bytes 24580
  246.6 1.1 copy-start.49
  246.6 39.5 %copy-start.37 = (f32[128]{0:T(128)S(1)}, f32[128]{0:T(128)}, u32[]{:S(2)}) copy-start(f32[128]{0:T(128)} %copy-done.34) | copy-start | bytes 1540
  246.6 39.5 %copy-start.47 = (f32[128]{0:T(128)S(1)}, f32[128]{0:T(128)}, u32[]{:S(2)}) copy-start(f32[128]{0:T(128)} %param.34) | copy-start | bytes 1540
  247.7 46.7 %copy-start.21 = (f32[9,8,16,128]{3,2,1,0:T(8,128)S(1)}, f32[9,8,16,128]{3,2,1,0:T(8,128)}, u32[]{:S(2)}) copy-start(f32[9,8,16,128]{3,2,1,0:T(8,128)} %get-tuple-element.1332) | copy-start | bytes 1769476
  286.7 5.6 %collective-permute-start.8 = (f32[8,16,1]{2,1,0:T(8,128)S(1)}, f32[8,16,1]{2,1,0:T(8,128)S(1)}, u32[]{:S(2)}, u32[]{:S(2)}) collective-permute-start(f32[8,16,1]{2,1,0:T(8,128)S(1)} %get-tuple-element.1371), channel_id=1, source_target_pairs={{0,16},{16,32},{32,48},{48,64},{64,80},{80,96},{96,112},{1,17},{17... | collective-permute-start | bytes 1544 | tf_op jit(solution)/shard_map/ppermute | solution.py:43
  288.6 5.5 %collective-permute-start.9 = (f32[8,16,1]{2,1,0:T(8,128)S(1)}, f32[8,16,1]{2,1,0:T(8,128)S(1)}, u32[]{:S(2)}, u32[]{:S(2)}) collective-permute-start(f32[8,16,1]{2,1,0:T(8,128)S(1)} %get-tuple-element.1372), channel_id=1, source_target_pairs={{16,0},{32,16},{48,32},{64,48},{80,64},{96,80},{112,96},{17,1},{33... | collective-permute-start | bytes 1544 | tf_op jit(solution)/shard_map/ppermute | solution.py:45
  295.3 2.6 copy-start.18
  302.2 0.8 slice-start.3
  304.0 0.8 copy-start.31
  306.1 21.1 %copy-start.5 = (f32[9,8,128]{2,1,0:T(8,128)S(1)}, f32[9,8,128]{2,1,0:T(8,128)}, u32[]{:S(2)}) copy-start(f32[9,8,128]{2,1,0:T(8,128)} %copy-done) | copy-start | bytes 110596
  334.2 24.1 %copy-start.13 = (f32[2,8,128]{2,1,0:T(8,128)S(1)}, f32[2,8,128]{2,1,0:T(8,128)}, u32[]{:S(2)}) copy-start(f32[2,8,128]{2,1,0:T(8,128)} %copy-done.8) | copy-start | bytes 24580
  360.1 5.6 %collective-permute-start.10 = (f32[8,16,1]{2,1,0:T(8,128)S(1)}, f32[8,16,1]{2,1,0:T(8,128)S(1)}, u32[]{:S(2)}, u32[]{:S(2)}) collective-permute-start(f32[8,16,1]{2,1,0:T(8,128)S(1)} %get-tuple-element.1361), channel_id=1, source_target_pairs={{0,16},{16,32},{32,48},{48,64},{64,80},{80,96},{96,112},{1,17},{17... | collective-permute-start | bytes 1544 | tf_op jit(solution)/shard_map/ppermute | solution.py:43
  362.0 5.5 %collective-permute-start.11 = (f32[8,16,1]{2,1,0:T(8,128)S(1)}, f32[8,16,1]{2,1,0:T(8,128)S(1)}, u32[]{:S(2)}, u32[]{:S(2)}) collective-permute-start(f32[8,16,1]{2,1,0:T(8,128)S(1)} %get-tuple-element.1362), channel_id=1, source_target_pairs={{16,0},{32,16},{48,32},{64,48},{80,64},{96,80},{112,96},{17,1},{33... | collective-permute-start | bytes 1544 | tf_op jit(solution)/shard_map/ppermute | solution.py:45
  368.7 2.6 copy-start.19
  375.6 0.8 slice-start.4
  377.4 0.8 copy-start.32
  379.5 21.1 %copy-start.6 = (f32[9,8,128]{2,1,0:T(8,128)S(1)}, f32[9,8,128]{2,1,0:T(8,128)}, u32[]{:S(2)}) copy-start(f32[9,8,128]{2,1,0:T(8,128)} %copy-done) | copy-start | bytes 110596
  407.6 23.9 %copy-start.14 = (f32[2,8,128]{2,1,0:T(8,128)S(1)}, f32[2,8,128]{2,1,0:T(8,128)}, u32[]{:S(2)}) copy-start(f32[2,8,128]{2,1,0:T(8,128)} %copy-done.8) | copy-start | bytes 24580
  432.7 5.6 %copy-start.39 = (f32[128]{0:T(128)S(1)}, f32[128]{0:T(128)}, u32[]{:S(2)}) copy-start(f32[128]{0:T(128)} %copy-done.34) | copy-start | bytes 1540
  432.7 5.6 %copy-start.43 = (f32[128]{0:T(128)S(1)}, f32[128]{0:T(128)}, u32[]{:S(2)}) copy-start(f32[128]{0:T(128)} %copy-done.41) | copy-start | bytes 1540
  432.7 5.6 %collective-permute-start.12 = (f32[8,16,1]{2,1,0:T(8,128)S(1)}, f32[8,16,1]{2,1,0:T(8,128)S(1)}, u32[]{:S(2)}, u32[]{:S(2)}) collective-permute-start(f32[8,16,1]{2,1,0:T(8,128)S(1)} %get-tuple-element.1351), channel_id=1, source_target_pairs={{0,16},{16,32},{32,48},{48,64},{64,80},{80,96},{96,112},{1,17},{17... | collective-permute-start | bytes 1544 | tf_op jit(solution)/shard_map/ppermute | solution.py:43
  434.6 5.5 %collective-permute-start.13 = (f32[8,16,1]{2,1,0:T(8,128)S(1)}, f32[8,16,1]{2,1,0:T(8,128)S(1)}, u32[]{:S(2)}, u32[]{:S(2)}) collective-permute-start(f32[8,16,1]{2,1,0:T(8,128)S(1)} %get-tuple-element.1352), channel_id=1, source_target_pairs={{16,0},{32,16},{48,32},{64,48},{80,64},{96,80},{112,96},{17,1},{33... | collective-permute-start | bytes 1544 | tf_op jit(solution)/shard_map/ppermute | solution.py:45
  441.2 2.6 copy-start.20
  447.5 0.8 slice-start.5
  450.8 21.1 %copy-start.1 = (f32[9,8,128]{2,1,0:T(8,128)S(1)}, f32[9,8,128]{2,1,0:T(8,128)}, u32[]{:S(2)}) copy-start(f32[9,8,128]{2,1,0:T(8,128)} %copy-done) | copy-start | bytes 110596
  478.9 23.9 %copy-start.9 = (f32[2,8,128]{2,1,0:T(8,128)S(1)}, f32[2,8,128]{2,1,0:T(8,128)}, u32[]{:S(2)}) copy-start(f32[2,8,128]{2,1,0:T(8,128)} %copy-done.8) | copy-start | bytes 24580
  504.4 38.7 %copy-start.33 = (f32[8,16,128]{2,1,0:T(8,128)}, f32[8,16,128]{2,1,0:T(8,128)S(1)}, u32[]{:S(2)}) copy-start(f32[8,16,128]{2,1,0:T(8,128)S(1)} %fusion.95) | copy-start | bytes 196612
  (8 other events, 4.9 us)
where the time goes:
time: 545 us; the launch traced here: 543 us
  blocking collectives  350 us (64%)
  local copies, waits for them, and re-layouts  74.5 us (14%)
  other arithmetic  51.7 us (9%)
  starting transfers between devices  39.3 us (7%)
  loops' own time  13.1 us (2%)
  waiting for transfers between devices  8.06 us (1%)
  between operations  6.37 us (1%)
    all_gather x12, blocking collectives, entering(): everything = lax.all_gather(shard, axis)  274 us
    psum x2, blocking collectives, on_device(): moment = lax.psum(partial_moment, 'depth')  76.4 us
    pad x36, local copies, waits for them, and re-layouts, forward_maps(): prefix = lax.associative_scan(forward_join, matrices, axis=2)  26.6 us
    ppermute x7, starting transfers between devices, with_halo(): lax.ppermute(head, axis, [((i + 1) % count, i) for i in range(ends)])  23.1 us
    slice x78, local copies, waits for them, and re-layouts, forward_maps(): prefix = lax.associative_scan(forward_join, matrices, axis=2)  20.4 us
    ppermute x7, starting transfers between devices, with_halo(): lax.ppermute(tail, axis, [(i, (i + 1) % count) for i in range(ends)])  16.2 us
    unnamed x136, local copies, waits for them, and re-layouts  15.2 us
    while x768, other arithmetic  13.4 us
  transfers between devices with their start and end apart: 14, of which 5 were waited for; matrix products, arithmetic and copies ran while one was open for 1% of the time, Pallas kernels for 0%

commit v1 on v0

v1 whole, which is shorter than its diff:
```python
import jax
import jax.numpy as jnp
from jax import lax
from jax.experimental import pallas as pl
from jax.experimental.pallas import tpu as pltpu
from jax.sharding import PartitionSpec as P

MESH = pl.DeviceIdType.MESH
F32 = jnp.float32

SOILS = 8
PANEL = 16
SUBSTEPS = 3
OUTER = 2
VNUM = 512.0
ALONG_RATE = 0.1
ACROSS_RATE = 0.06
SPRING_KEEP = 0.5
SPRING_DRIVE = 2.0

CROSS = 8
ROWS = 16
BLOCKS = 16
OWN = 8
WIDE = 3 * OWN
GROUPS = 3
LANES = 128
LAST = ROWS - 1
MIDDLE = 7
LAYER, PRESSURE, LOADING = 0, 1, 2


def lane_roll(x, shift):
    return pltpu.roll(x, shift % LANES, x.ndim - 1)


def cross_roll(x, shift):
    return pltpu.roll(x, shift % CROSS, x.ndim - 2)


def harmonic(a, b):
    return (2.0 * VNUM) * a * b / (a + b)


def pick(level, table, row):
    value = jnp.full(level.shape, table[row, 0], F32)
    for soil in range(1, SOILS):
        value = jnp.where(level == float(soil), table[row, soil], value)
    return value


def kernel(
    table, contact, pressure, layer, loading, spring,
    pressure_out, spring_out,
    packed, landed, nothing, wall_mine, wall_beside,
    field, source, keep, along, back, ahead, chain, outward, from_prev, from_last,
    reduce_up, reduce_down, reduced_inv, sep_up, sep_down, springs,
    result, returned, spring_row, spring_rows,
    send_sem, land_sem, wall_sem, wall_send, return_send, return_sem, row_send, row_sem,
):
    wall, me = lax.axis_index("wall"), lax.axis_index("depth")
    walls = lax.axis_size("wall")
    has_left, has_right = wall > 0, wall < walls - 1
    first, last = me == 0, me == BLOCKS - 1

    barrier = pltpu.get_barrier_semaphore()

    def greet(k, _):
        pl.semaphore_signal(
            barrier, inc=1, device_id=(wall, lax.rem(me + k, BLOCKS)), device_id_type=MESH
        )
        return 0

    lax.fori_loop(1, BLOCKS, greet, 0)

    @pl.when(first & has_left)
    def _():
        def call(k, _):
            pl.semaphore_signal(barrier, inc=1, device_id=(wall - 1, k), device_id_type=MESH)
            return 0

        lax.fori_loop(0, BLOCKS, call, 0)

    @pl.when(last & has_right)
    def _():
        def call(k, _):
            pl.semaphore_signal(barrier, inc=1, device_id=(wall + 1, k), device_id_type=MESH)
            return 0

        lax.fori_loop(0, BLOCKS, call, 0)

    for which, ref in ((LAYER, layer), (PRESSURE, pressure), (LOADING, loading)):
        flat = ref.reshape(CROSS * ROWS, LANES)
        planes = [flat[pl.ds(z, CROSS, stride=ROWS), :] for z in range(ROWS)]
        packed[which] = jnp.concatenate(planes, 0).astype(F32).T

    lane = lax.broadcasted_iota(jnp.int32, (8, LANES), 1)
    sub = lax.broadcasted_iota(jnp.int32, (8, LANES), 0)
    share = jnp.zeros((8, LANES), F32)
    for panel in range(LANES // PANEL):
        share = jnp.where(lane // PANEL == panel, contact[panel].astype(F32), share)
    own_spring = jnp.broadcast_to(spring[...].reshape(1, LANES), (8, LANES))
    wall_mine[...] = jnp.where(sub == 0, own_spring, share)

    sides = has_left.astype(jnp.int32) + has_right.astype(jnp.int32)
    pl.semaphore_wait(barrier, BLOCKS - 1 + sides)

    def to_peer(which, to, start, size, at, slot):
        return pltpu.make_async_remote_copy(
            src_ref=packed.at[which, pl.ds(start, size)],
            dst_ref=landed.at[which, me, pl.ds(at, size)],
            send_sem=send_sem.at[which, slot],
            recv_sem=land_sem.at[which],
            device_id=to,
            device_id_type=MESH,
        )

    def to_self(which, start, size, at):
        return pltpu.make_async_copy(
            packed.at[which, pl.ds(start, size)],
            landed.at[which, me, pl.ds(at, size)],
            land_sem.at[which],
        )

    def no_column(which, at):
        return pltpu.make_async_copy(
            nothing, landed.at[which, :, pl.ds(at, OWN)], land_sem.at[which]
        )

    def for_each_copy(which, act):
        def deal(k, _):
            to = lax.rem(me + k, BLOCKS)

            @pl.when(to == 0)
            def _():
                act(to_peer(which, (wall, to), 0, 2 * OWN, OWN, k))

            @pl.when(to == BLOCKS - 1)
            def _():
                act(to_peer(which, (wall, to), LANES - 2 * OWN, 2 * OWN, 0, k))

            @pl.when((to > 0) & (to < BLOCKS - 1))
            def _():
                start = pl.multiple_of((to - 1) * OWN, OWN)
                act(to_peer(which, (wall, to), start, WIDE, 0, k))

            return 0

        lax.fori_loop(1, BLOCKS, deal, 0)

        @pl.when(has_right)
        def _():
            act(to_peer(which, (wall + 1, 0), LANES - OWN, OWN, 0, BLOCKS))

        @pl.when(has_left)
        def _():
            act(to_peer(which, (wall - 1, BLOCKS - 1), 0, OWN, 2 * OWN, 0))

    to_right = pltpu.make_async_remote_copy(
        src_ref=wall_mine, dst_ref=wall_beside, send_sem=wall_send.at[0], recv_sem=wall_sem.at[0],
        device_id=(wall + 1, 0), device_id_type=MESH,
    )
    to_left = pltpu.make_async_remote_copy(
        src_ref=wall_mine, dst_ref=wall_beside, send_sem=wall_send.at[1], recv_sem=wall_sem.at[0],
        device_id=(wall - 1, BLOCKS - 1), device_id_type=MESH,
    )
    nothing[...] = jnp.zeros_like(nothing)
    for which in (LAYER, PRESSURE, LOADING):
        for_each_copy(which, lambda copy: copy.start())

        @pl.when(first)
        def _():
            to_self(which, 0, 2 * OWN, OWN).start()

        @pl.when(last)
        def _():
            to_self(which, LANES - 2 * OWN, 2 * OWN, 0).start()

        @pl.when(jnp.logical_not(first | last))
        def _():
            to_self(which, pl.multiple_of((me - 1) * OWN, OWN), WIDE, 0).start()

        @pl.when(first & jnp.logical_not(has_left))
        def _():
            no_column(which, 0).start()

        @pl.when(last & jnp.logical_not(has_right))
        def _():
            no_column(which, 2 * OWN).start()

    @pl.when(first & has_right)
    def _():
        to_right.start()

    @pl.when(last & has_left)
    def _():
        to_left.start()

    wide = (GROUPS, CROSS, LANES)
    lanes = lax.broadcasted_iota(jnp.int32, wide, 2)
    block = lanes // OWN
    column = 3 * (lanes % OWN) + lax.broadcasted_iota(jnp.int32, wide, 0)
    cross = lax.broadcasted_iota(jnp.int32, wide, 1)
    place = wall * LANES + me * OWN - OWN + column
    inside = (place >= 0) & (place < walls * LANES)
    top, bottom = block == 0, block == BLOCKS - 1

    def arrived(which):
        pltpu.make_async_copy(landed.at[which], landed.at[which], land_sem.at[which]).wait()
        for g in range(GROUPS):
            rows = [landed[which, s, pl.ds(g, OWN, stride=GROUPS), :] for s in range(BLOCKS)]
            turned = jnp.concatenate(rows, 0).T.reshape(ROWS, CROSS, LANES)
            field_or = source if which == LOADING else field
            field_or[:, g] = turned

    arrived(LAYER)
    perm = [pick(field[z], table, 0) for z in range(ROWS)]
    up = [None] * ROWS
    for z in range(1, ROWS):
        up[z] = harmonic(perm[z - 1], perm[z])
    up[0] = jnp.where(top, VNUM * perm[0], harmonic(lane_roll(perm[LAST], OWN), perm[0]))
    down = up[1:] + [jnp.where(bottom, 0.0, lane_roll(up[0], -OWN))]
    diagonal = [1.0 + up[z] + down[z] for z in range(ROWS)]

    inverse, toward = [None] * ROWS, [None] * ROWS
    chained = [None] * ROWS
    for z in range(MIDDLE):
        pivot = diagonal[z] if z == 0 else diagonal[z] - up[z] * toward[z - 1]
        inverse[z] = 1.0 / pivot
        toward[z] = down[z] * inverse[z]
        chained[z] = up[z] * inverse[z]
    for z in range(LAST - 1, MIDDLE, -1):
        pivot = diagonal[z] if z == LAST - 1 else diagonal[z] - down[z] * toward[z + 1]
        inverse[z] = 1.0 / pivot
        toward[z] = up[z] * inverse[z]
        chained[z] = down[z] * inverse[z]
    inverse[MIDDLE] = 1.0 / (
        diagonal[MIDDLE] - up[MIDDLE] * toward[MIDDLE - 1] - down[MIDDLE] * toward[MIDDLE + 1]
    )
    chained[MIDDLE] = up[MIDDLE] * inverse[MIDDLE]
    toward[MIDDLE] = down[MIDDLE] * inverse[MIDDLE]
    inverse[LAST] = jnp.ones(wide, F32)

    upper, lower = [None] * LAST, [None] * LAST
    upper[0] = jnp.where(top, 0.0, chained[0])
    for z in range(1, MIDDLE):
        upper[z] = chained[z] * upper[z - 1]
    upper[MIDDLE] = chained[MIDDLE] * upper[MIDDLE - 1]
    for z in range(MIDDLE - 1, -1, -1):
        upper[z] = upper[z] + toward[z] * upper[z + 1]
    for z in range(MIDDLE + 1, LAST):
        upper[z] = toward[z] * upper[z - 1]
    lower[LAST - 1] = chained[LAST - 1]
    for z in range(LAST - 2, MIDDLE, -1):
        lower[z] = chained[z] * lower[z + 1]
    lower[MIDDLE] = toward[MIDDLE] * lower[MIDDLE + 1]
    for z in range(MIDDLE + 1, LAST):
        lower[z] = lower[z] + toward[z] * lower[z - 1]
    for z in range(MIDDLE - 1, -1, -1):
        lower[z] = toward[z] * lower[z + 1]
    for z in range(LAST):
        chain[z], outward[z] = chained[z], toward[z]
        from_prev[z], from_last[z] = upper[z], lower[z]

    a_coef = up[LAST] * upper[LAST - 1]
    c_coef = down[LAST] * lane_roll(lower[0], -OWN)
    b_coef = diagonal[LAST] - up[LAST] * lower[LAST - 1] - down[LAST] * lane_roll(upper[0], -OWN)
    sep_up[...], sep_down[...] = up[LAST], down[LAST]
    for level in range(4):
        hop = OWN << level
        b_inv = 1.0 / b_coef
        alpha = a_coef * lane_roll(b_inv, hop)
        gamma = c_coef * lane_roll(b_inv, -hop)
        reduce_up[level], reduce_down[level] = alpha, gamma
        b_coef = b_coef - alpha * lane_roll(c_coef, hop) - gamma * lane_roll(a_coef, -hop)
        a_coef, c_coef = alpha * lane_roll(a_coef, hop), gamma * lane_roll(c_coef, -hop)
    reduced_inv[...] = 1.0 / b_coef

    @pl.when((first & has_left) | (last & has_right))
    def _():
        pltpu.make_async_copy(wall_beside, wall_beside, wall_sem.at[0]).wait()

    @pl.when(jnp.logical_not((first & has_left) | (last & has_right)))
    def _():
        wall_beside[...] = jnp.zeros_like(wall_beside)

    beside = (first & (lane >= LANES - OWN)) | (last & (lane < OWN))
    window = jnp.where(beside, wall_beside[...], wall_mine[...])
    window = lane_roll_by(window, lax.rem(LANES + OWN - me * OWN, LANES))
    touching = []
    for g in range(GROUPS):
        spread = jnp.take_along_axis(window, 3 * (lane % OWN) + g, axis=1)
        springs[g] = jnp.broadcast_to(spread[0:1], (CROSS, LANES))
        touching.append(jnp.broadcast_to(spread[1:2], (CROSS, LANES)))
    touching = jnp.stack(touching)

    ahead_mask = (cross < CROSS - 1).astype(F32)
    back_mask = jnp.where(cross > 0, 1.0, touching)
    for z in range(ROWS):
        lateral = jnp.where(inside, pick(field[z], table, 1), 0.0)
        a1 = ALONG_RATE * lateral
        a2 = ACROSS_RATE * lateral
        a2b, a2a = a2 * back_mask, a2 * ahead_mask
        keep[z] = (1.0 - 2.0 * a1 - a2b - a2a) * inverse[z]
        along[z], back[z], ahead[z] = a1 * inverse[z], a2b * inverse[z], a2a * inverse[z]
    arrived(LOADING)
    for z in range(ROWS):
        source[z] = source[z] * inverse[z]
    arrived(PRESSURE)

    def solve(_, carry):
        spring_now = springs[...]
        scaled = []
        for z in range(ROWS):
            now = field[z]
            left = jnp.stack([lane_roll(now[2], 1), now[0], now[1]])
            right = jnp.stack([now[1], now[2], lane_roll(now[0], -1)])
            behind = jnp.where(cross == 0, spring_now, cross_roll(now, 1))
            scaled.append(
                source[z] + keep[z] * now + along[z] * (left + right)
                + back[z] * behind + ahead[z] * cross_roll(now, -1)
            )
        for z in range(1, MIDDLE):
            scaled[z] = scaled[z] + chain[z] * scaled[z - 1]
        for z in range(LAST - 2, MIDDLE, -1):
            scaled[z] = scaled[z] + chain[z] * scaled[z + 1]
        scaled[MIDDLE] = (
            scaled[MIDDLE] + chain[MIDDLE] * scaled[MIDDLE - 1] + outward[MIDDLE] * scaled[MIDDLE + 1]
        )
        for z in range(MIDDLE - 1, -1, -1):
            scaled[z] = scaled[z] + outward[z] * scaled[z + 1]
        for z in range(MIDDLE + 1, LAST):
            scaled[z] = scaled[z] + outward[z] * scaled[z - 1]
        ends = (
            scaled[LAST] + sep_up[...] * scaled[LAST - 1]
            + sep_down[...] * lane_roll(scaled[0], -OWN)
        )
        for level in range(4):
            hop = OWN << level
            ends = (
                ends + reduce_up[level] * lane_roll(ends, hop)
                + reduce_down[level] * lane_roll(ends, -hop)
            )
        ends = ends * reduced_inv[...]
        above = lane_roll(ends, OWN)
        for z in range(LAST):
            field[z] = scaled[z] + from_prev[z] * above + from_last[z] * ends
        field[LAST] = ends
        return carry

    def outer_step(_, carry):
        lax.fori_loop(0, SUBSTEPS, solve, 0)
        base = ROWS * block.astype(F32) + 0.5
        moment = jnp.zeros(wide, F32)
        for z in range(ROWS):
            moment = moment + (base + float(z)) * field[z]
        for level in range(4):
            moment = moment + lane_roll(moment, OWN << level)
        moment = moment * (1.0 / (ROWS * BLOCKS) ** 2)
        springs[...] = SPRING_KEEP * springs[...] + SPRING_DRIVE * touching * moment
        return carry

    lax.fori_loop(0, OUTER, outer_step, 0)

    spot = lane % OWN

    def own_columns(planes):
        out = jnp.zeros((8, LANES), F32)
        for place_here in range(OWN):
            at, g = divmod(OWN + place_here, GROUPS)
            out = jnp.where(spot == place_here, lane_roll(planes[g], place_here - at), out)
        return out

    mine = jnp.concatenate([own_columns(field[z]) for z in range(ROWS)], 0)
    result[...] = mine.T.reshape(BLOCKS, OWN, LANES)
    spring_row[...] = own_columns(springs[...])[0:1]

    def give_back(k):
        to = lax.rem(me + k, BLOCKS)
        planes = pltpu.make_async_remote_copy(
            src_ref=result.at[to], dst_ref=returned.at[me],
            send_sem=return_send.at[k], recv_sem=return_sem.at[0],
            device_id=(wall, to), device_id_type=MESH,
        )
        row = pltpu.make_async_remote_copy(
            src_ref=spring_row, dst_ref=spring_rows.at[me],
            send_sem=row_send.at[k], recv_sem=row_sem.at[0],
            device_id=(wall, to), device_id_type=MESH,
        )
        return planes, row

    def start_back(k, _):
        planes, row = give_back(k)
        planes.start()
        row.start()
        return 0

    lax.fori_loop(1, BLOCKS, start_back, 0)
    pltpu.make_async_copy(result.at[me], returned.at[me], return_sem.at[0]).start()
    pltpu.make_async_copy(spring_row, spring_rows.at[me], row_sem.at[0]).start()

    for which in (LAYER, PRESSURE, LOADING):
        for_each_copy(which, lambda copy: copy.wait_send())

    @pl.when(first & has_right)
    def _():
        to_right.wait_send()

    @pl.when(last & has_left)
    def _():
        to_left.wait_send()

    pltpu.make_async_copy(returned, returned, return_sem.at[0]).wait()
    final = returned[...].reshape(LANES, LANES).T
    flat_out = pressure_out.reshape(CROSS * ROWS, LANES)
    for z in range(ROWS):
        flat_out[pl.ds(z, CROSS, stride=ROWS), :] = final[z * CROSS:(z + 1) * CROSS]

    pltpu.make_async_copy(spring_rows, spring_rows, row_sem.at[0]).wait()
    total = jnp.zeros((1, LANES), F32)
    for d in range(BLOCKS):
        total = jnp.where(lane[0:1] // OWN == d, spring_rows[d], total)
    spring_out[...] = total.reshape(spring_out.shape)

    def finish_back(k, _):
        planes, row = give_back(k)
        planes.wait_send()
        row.wait_send()
        return 0

    lax.fori_loop(1, BLOCKS, finish_back, 0)


def lane_roll_by(x, shift):
    return pltpu.roll(x, shift, x.ndim - 1)


def on_device(pressure, layer, permeability, loading, spring, contact):
    vmem = pl.BlockSpec(memory_space=pltpu.VMEM)
    smem = pl.BlockSpec(memory_space=pltpu.SMEM)
    planes = pltpu.VMEM((ROWS, GROUPS, CROSS, LANES), F32)
    plane = pltpu.VMEM((GROUPS, CROSS, LANES), F32)
    steps = pltpu.VMEM((4, GROUPS, CROSS, LANES), F32)
    tile = pltpu.VMEM((8, LANES), F32)
    return pl.pallas_call(
        kernel,
        out_shape=(
            jax.ShapeDtypeStruct(pressure.shape, F32),
            jax.ShapeDtypeStruct(spring.shape, F32),
        ),
        in_specs=[smem, smem, vmem, vmem, vmem, vmem],
        out_specs=(vmem, vmem),
        scratch_shapes=[
            pltpu.VMEM((3, LANES, LANES), F32),
            pltpu.VMEM((3, BLOCKS, WIDE, LANES), F32),
            pltpu.VMEM((BLOCKS, OWN, LANES), F32),
            tile, tile,
            planes, planes, planes, planes, planes, planes,
            planes, planes, planes, planes,
            steps, steps, plane, plane, plane, plane,
            pltpu.VMEM((BLOCKS, OWN, LANES), F32),
            pltpu.VMEM((BLOCKS, OWN, LANES), F32),
            pltpu.VMEM((1, LANES), F32),
            pltpu.VMEM((BLOCKS, 1, LANES), F32),
            pltpu.SemaphoreType.DMA((3, BLOCKS + 1)),
            pltpu.SemaphoreType.DMA((3,)),
            pltpu.SemaphoreType.DMA((1,)),
            pltpu.SemaphoreType.DMA((2,)),
            pltpu.SemaphoreType.DMA((BLOCKS,)),
            pltpu.SemaphoreType.DMA((1,)),
            pltpu.SemaphoreType.DMA((BLOCKS,)),
            pltpu.SemaphoreType.DMA((1,)),
        ],
        compiler_params=pltpu.CompilerParams(
            collective_id=0, has_side_effects=True, vmem_limit_bytes=24 << 20
        ),
    )(permeability, contact, pressure, layer, loading, spring)


def solution(mesh):
    cells = P(None, "depth", "wall")
    return jax.shard_map(
        on_device,
        mesh=mesh,
        in_specs=(cells, cells, P(), cells, P("wall"), P("wall")),
        out_specs=(cells, P("wall")),
        check_vma=False,
    )
```

time: 545 us -> 34.3 us (0.06)
  the two profiles are of different devices: /device:TPU:96 before, /device:TPU:1 now
where the time goes in v1:
time: 34.3 us; the launch traced here: 34 us
  Pallas kernels  27.7 us (81%)
  local copies, waits for them, and re-layouts  5.64 us (16%)
  between operations  0.65 us (2%)
    pallas_call x1, Pallas kernels, on_device(): pl.pallas_call(kernel, out_shape=(jax.ShapeDtypeStruct(pressure.shape, F3...  27.7 us
    unnamed x14, local copies, waits for them, and re-layouts  5.64 us

profile of v1, /device:TPU:1, one launch (start us, length us, event | category | flops | bytes accessed | tf_op | source)
XLA Modules:
  0.0 34.0 jit_solution(10594433130817542224)
XLA Ops:
  0.6 0.0 copy-start
  0.6 0.8 %copy-done = f32[8,16,128]{2,1,0:T(8,128)S(1)} copy-done((f32[8,16,128]{2,1,0:T(8,128)S(1)}, f32[8,16,128]{2,1,0:T(8,128)}, u32[]{:S(2)}) %copy-start) | copy-done | bytes 65560
  1.5 0.0 copy-start.1
  1.5 0.8 %copy-done.1 = s32[8,16,128]{2,1,0:T(8,128)S(1)} copy-done((s32[8,16,128]{2,1,0:T(8,128)S(1)}, s32[8,16,128]{2,1,0:T(8,128)}, u32[]{:S(2)}) %copy-start.1) | copy-done | bytes 65560
  2.3 0.0 copy-start.2
  2.3 0.8 %copy-done.2 = f32[8,16,128]{2,1,0:T(8,128)S(1)} copy-done((f32[8,16,128]{2,1,0:T(8,128)S(1)}, f32[8,16,128]{2,1,0:T(8,128)}, u32[]{:S(2)}) %copy-start.2) | copy-done | bytes 65560
  3.2 0.0 copy-start.3
  3.2 0.7 %copy-done.3 = f32[2,8]{1,0:T(2,128)S(1)} copy-done((f32[2,8]{1,0:T(2,128)S(1)}, f32[2,8]{1,0:T(2,128)}, u32[]{:S(2)}) %copy-start.3) | copy-done | bytes 88
  3.8 0.0 copy-start.4
  3.8 0.7 %copy-done.4 = s32[8]{0:T(128)S(1)} copy-done((s32[8]{0:T(128)S(1)}, s32[8]{0:T(128)}, u32[]{:S(2)}) %copy-start.4) | copy-done | bytes 56
  4.5 0.0 copy-start.5
  4.5 0.7 %copy-done.5 = f32[128]{0:T(128)S(1)} copy-done((f32[128]{0:T(128)S(1)}, f32[128]{0:T(128)}, u32[]{:S(2)}) %copy-start.5) | copy-done | bytes 536
  5.1 27.7 %shard_map.77 = (f32[8,16,128]{2,1,0:T(8,128)S(1)}, f32[128]{0:T(128)S(1)}) custom-call(f32[2,8]{1,0:T(2,128)S(1)} %copy-done.3, s32[8]{0:T(128)S(1)} %copy-done.4, f32[8,16,128]{2,1,0:T(8,128)S(1)} %copy-done, s32[8,16,128]{2,1,0:T(8,128)S(1)} %copy-done.1, f32[8,16,128]{2,1,0:T(8,128)S(1)} %copy-done.2, f32[128]{0:T(128)S(1)} %copy-done.5), custom_call_target="tpu_custom_call" | custom-call | tf_op jit(solution)/shard_map/pallas_call | solution.py:445
  32.9 0.6 %copy.10 = f32[8,16,128]{2,1,0:T(8,128)} copy(f32[8,16,128]{2,1,0:T(8,128)S(1)} %get-tuple-element.4) | data formatting | bytes 131072
  33.5 0.5 %copy.11 = f32[128]{0:T(128)} copy(f32[128]{0:T(128)S(1)} %get-tuple-element.5) | data formatting | bytes 1024
Async XLA Ops:
  0.6 0.8 %copy-start = (f32[8,16,128]{2,1,0:T(8,128)S(1)}, f32[8,16,128]{2,1,0:T(8,128)}, u32[]{:S(2)}) copy-start(f32[8,16,128]{2,1,0:T(8,128)} %pressure.1) | copy-start | bytes 196612
  1.5 0.8 %copy-start.1 = (s32[8,16,128]{2,1,0:T(8,128)S(1)}, s32[8,16,128]{2,1,0:T(8,128)}, u32[]{:S(2)}) copy-start(s32[8,16,128]{2,1,0:T(8,128)} %layer.1) | copy-start | bytes 196612
  2.3 0.8 %copy-start.2 = (f32[8,16,128]{2,1,0:T(8,128)S(1)}, f32[8,16,128]{2,1,0:T(8,128)}, u32[]{:S(2)}) copy-start(f32[8,16,128]{2,1,0:T(8,128)} %loading.1) | copy-start | bytes 196612
  3.2 0.7 %copy-start.3 = (f32[2,8]{1,0:T(2,128)S(1)}, f32[2,8]{1,0:T(2,128)}, u32[]{:S(2)}) copy-start(f32[2,8]{1,0:T(2,128)} %table.1) | copy-start | bytes 196
  3.8 0.7 %copy-start.4 = (s32[8]{0:T(128)S(1)}, s32[8]{0:T(128)}, u32[]{:S(2)}) copy-start(s32[8]{0:T(128)} %contact.1) | copy-start | bytes 100
  4.5 0.7 %copy-start.5 = (f32[128]{0:T(128)S(1)}, f32[128]{0:T(128)}, u32[]{:S(2)}) copy-start(f32[128]{0:T(128)} %spring.1) | copy-start | bytes 1540

commit v2 on v1

--- a/solution.py
+++ b/solution.py
@@ -28,6 +28,8 @@
 LAST = ROWS - 1
 MIDDLE = 7
 LAYER, PRESSURE, LOADING = 0, 1, 2
+HALO = (5, 6, 5)
+SENT = OWN + 1
 
 
 def lane_roll(x, shift):
@@ -50,19 +52,30 @@
 
 
 def kernel(
-    table, contact, pressure, layer, loading, spring,
-    pressure_out, spring_out,
+    table_in, contact_in, pressure_in, layer_in, loading_in, spring_in,
+    returned,
+    table, contact, pressure, layer, loading, spring, in_sem,
     packed, landed, nothing, wall_mine, wall_beside,
     field, source, keep, along, back, ahead, chain, outward, from_prev, from_last,
     reduce_up, reduce_down, reduced_inv, sep_up, sep_down, springs,
-    result, returned, spring_row, spring_rows,
-    send_sem, land_sem, wall_sem, wall_send, return_send, return_sem, row_send, row_sem,
+    result,
+    send_sem, land_sem, wall_sem, wall_send, return_send, return_sem,
 ):
     wall, me = lax.axis_index("wall"), lax.axis_index("depth")
     walls = lax.axis_size("wall")
     has_left, has_right = wall > 0, wall < walls - 1
     first, last = me == 0, me == BLOCKS - 1
 
+    inputs = [
+        pltpu.make_async_copy(source_ref, here, in_sem.at[at])
+        for at, (source_ref, here) in enumerate((
+            (layer_in, layer), (pressure_in, pressure), (loading_in, loading),
+            (spring_in, spring), (contact_in, contact), (table_in, table),
+        ))
+    ]
+    for copy in inputs:
+        copy.start()
+
     barrier = pltpu.get_barrier_semaphore()
 
     def greet(k, _):
@@ -89,21 +102,11 @@
 
         lax.fori_loop(0, BLOCKS, call, 0)
 
-    for which, ref in ((LAYER, layer), (PRESSURE, pressure), (LOADING, loading)):
+    def pack(which, ref):
+        inputs[which].wait()
         flat = ref.reshape(CROSS * ROWS, LANES)
         planes = [flat[pl.ds(z, CROSS, stride=ROWS), :] for z in range(ROWS)]
         packed[which] = jnp.concatenate(planes, 0).astype(F32).T
-
-    lane = lax.broadcasted_iota(jnp.int32, (8, LANES), 1)
-    sub = lax.broadcasted_iota(jnp.int32, (8, LANES), 0)
-    share = jnp.zeros((8, LANES), F32)
-    for panel in range(LANES // PANEL):
-        share = jnp.where(lane // PANEL == panel, contact[panel].astype(F32), share)
-    own_spring = jnp.broadcast_to(spring[...].reshape(1, LANES), (8, LANES))
-    wall_mine[...] = jnp.where(sub == 0, own_spring, share)
-
-    sides = has_left.astype(jnp.int32) + has_right.astype(jnp.int32)
-    pl.semaphore_wait(barrier, BLOCKS - 1 + sides)
 
     def to_peer(which, to, start, size, at, slot):
         return pltpu.make_async_remote_copy(
@@ -122,27 +125,28 @@
             land_sem.at[which],
         )
 
-    def no_column(which, at):
+    def no_column(which, size, at):
         return pltpu.make_async_copy(
-            nothing, landed.at[which, :, pl.ds(at, OWN)], land_sem.at[which]
+            nothing.at[:, pl.ds(0, size)], landed.at[which, :, pl.ds(at, size)], land_sem.at[which]
         )
 
     def for_each_copy(which, act):
+        halo = HALO[which]
+
         def deal(k, _):
             to = lax.rem(me + k, BLOCKS)
 
             @pl.when(to == 0)
             def _():
-                act(to_peer(which, (wall, to), 0, 2 * OWN, OWN, k))
+                act(to_peer(which, (wall, to), 0, OWN + halo, OWN, k))
 
             @pl.when(to == BLOCKS - 1)
             def _():
-                act(to_peer(which, (wall, to), LANES - 2 * OWN, 2 * OWN, 0, k))
+                act(to_peer(which, (wall, to), LANES - OWN - halo, OWN + halo, OWN - halo, k))
 
             @pl.when((to > 0) & (to < BLOCKS - 1))
             def _():
-                start = pl.multiple_of((to - 1) * OWN, OWN)
-                act(to_peer(which, (wall, to), start, WIDE, 0, k))
+                act(to_peer(which, (wall, to), to * OWN - halo, OWN + 2 * halo, OWN - halo, k))
 
             return 0
 
@@ -150,12 +154,55 @@
 
         @pl.when(has_right)
         def _():
-            act(to_peer(which, (wall + 1, 0), LANES - OWN, OWN, 0, BLOCKS))
+            act(to_peer(which, (wall + 1, 0), LANES - halo, halo, OWN - halo, BLOCKS))
 
         @pl.when(has_left)
         def _():
-            act(to_peer(which, (wall - 1, BLOCKS - 1), 0, OWN, 2 * OWN, 0))
-
+            act(to_peer(which, (wall - 1, BLOCKS - 1), 0, halo, 2 * OWN, 0))
+
+    def deal_out(which):
+        halo = HALO[which]
+        for_each_copy(which, lambda copy: copy.start())
+
+        @pl.when(first)
+        def _():
+            to_self(which, 0, OWN + halo, OWN).start()
+
+        @pl.when(last)
+        def _():
+            to_self(which, LANES - OWN - halo, OWN + halo, OWN - halo).start()
+
+        @pl.when(jnp.logical_not(first | last))
+        def _():
+            to_self(which, me * OWN - halo, OWN + 2 * halo, OWN - halo).start()
+
+        @pl.when(first & jnp.logical_not(has_left))
+        def _():
+            no_column(which, halo, OWN - halo).start()
+
+        @pl.when(last & jnp.logical_not(has_right))
+        def _():
+            no_column(which, halo, 2 * OWN).start()
+
+    pack(LAYER, layer)
+    nothing[...] = jnp.zeros_like(nothing)
+    sides = has_left.astype(jnp.int32) + has_right.astype(jnp.int32)
+    pl.semaphore_wait(barrier, BLOCKS - 1 + sides)
+    deal_out(LAYER)
+    pack(PRESSURE, pressure)
+    deal_out(PRESSURE)
+    pack(LOADING, loading)
+    deal_out(LOADING)
+
+    for copy in inputs[LOADING + 1:]:
+        copy.wait()
+    lane = lax.broadcasted_iota(jnp.int32, (8, LANES), 1)
+    sub = lax.broadcasted_iota(jnp.int32, (8, LANES), 0)
+    share = jnp.zeros((8, LANES), F32)
+    for panel in range(LANES // PANEL):
+        share = jnp.where(lane // PANEL == panel, contact[panel].astype(F32), share)
+    own_spring = jnp.broadcast_to(spring[...].reshape(1, LANES), (8, LANES))
+    wall_mine[...] = jnp.where(sub == 0, own_spring, share)
     to_right = pltpu.make_async_remote_copy(
         src_ref=wall_mine, dst_ref=wall_beside, send_sem=wall_send.at[0], recv_sem=wall_sem.at[0],
         device_id=(wall + 1, 0), device_id_type=MESH,
@@ -164,29 +211,6 @@
         src_ref=wall_mine, dst_ref=wall_beside, send_sem=wall_send.at[1], recv_sem=wall_sem.at[0],
         device_id=(wall - 1, BLOCKS - 1), device_id_type=MESH,
     )
-    nothing[...] = jnp.zeros_like(nothing)
-    for which in (LAYER, PRESSURE, LOADING):
-        for_each_copy(which, lambda copy: copy.start())
-
-        @pl.when(first)
-        def _():
-            to_self(which, 0, 2 * OWN, OWN).start()
-
-        @pl.when(last)
-        def _():
-            to_self(which, LANES - 2 * OWN, 2 * OWN, 0).start()
-
-        @pl.when(jnp.logical_not(first | last))
-        def _():
-            to_self(which, pl.multiple_of((me - 1) * OWN, OWN), WIDE, 0).start()
-
-        @pl.when(first & jnp.logical_not(has_left))
-        def _():
-            no_column(which, 0).start()
-
-        @pl.when(last & jnp.logical_not(has_right))
-        def _():
-            no_column(which, 2 * OWN).start()
 
     @pl.when(first & has_right)
     def _():
@@ -206,7 +230,8 @@
     top, bottom = block == 0, block == BLOCKS - 1
 
     def arrived(which):
-        pltpu.make_async_copy(landed.at[which], landed.at[which], land_sem.at[which]).wait()
+        valid = landed.at[which, :, pl.ds(OWN - HALO[which], OWN + 2 * HALO[which])]
+        pltpu.make_async_copy(valid, valid, land_sem.at[which]).wait()
         for g in range(GROUPS):
             rows = [landed[which, s, pl.ds(g, OWN, stride=GROUPS), :] for s in range(BLOCKS)]
             turned = jnp.concatenate(rows, 0).T.reshape(ROWS, CROSS, LANES)
@@ -372,32 +397,25 @@
         return out
 
     mine = jnp.concatenate([own_columns(field[z]) for z in range(ROWS)], 0)
-    result[...] = mine.T.reshape(BLOCKS, OWN, LANES)
-    spring_row[...] = own_columns(springs[...])[0:1]
+    result[:, 0:OWN] = mine.T.reshape(BLOCKS, OWN, LANES)
+    result[:, OWN:] = jnp.broadcast_to(own_columns(springs[...])[None], (BLOCKS, 8, LANES))
 
     def give_back(k):
         to = lax.rem(me + k, BLOCKS)
-        planes = pltpu.make_async_remote_copy(
-            src_ref=result.at[to], dst_ref=returned.at[me],
+        return pltpu.make_async_remote_copy(
+            src_ref=result.at[to, pl.ds(0, SENT)], dst_ref=returned.at[me, pl.ds(0, SENT)],
             send_sem=return_send.at[k], recv_sem=return_sem.at[0],
             device_id=(wall, to), device_id_type=MESH,
         )
-        row = pltpu.make_async_remote_copy(
-            src_ref=spring_row, dst_ref=spring_rows.at[me],
-            send_sem=row_send.at[k], recv_sem=row_sem.at[0],
-            device_id=(wall, to), device_id_type=MESH,
-        )
-        return planes, row
 
     def start_back(k, _):
-        planes, row = give_back(k)
-        planes.start()
-        row.start()
+        give_back(k).start()
         return 0
 
     lax.fori_loop(1, BLOCKS, start_back, 0)
-    pltpu.make_async_copy(result.at[me], returned.at[me], return_sem.at[0]).start()
-    pltpu.make_async_copy(spring_row, spring_rows.at[me], row_sem.at[0]).start()
+    pltpu.make_async_copy(
+        result.at[me, pl.ds(0, SENT)], returned.at[me, pl.ds(0, SENT)], return_sem.at[0]
+    ).start()
 
     for which in (LAYER, PRESSURE, LOADING):
         for_each_copy(which, lambda copy: copy.wait_send())
@@ -410,25 +428,25 @@
     def _():
         to_left.wait_send()
 
-    pltpu.make_async_copy(returned, returned, return_sem.at[0]).wait()
-    final = returned[...].reshape(LANES, LANES).T
-    flat_out = pressure_out.reshape(CROSS * ROWS, LANES)
+    def finish_back(k, _):
+        give_back(k).wait_send()
+        return 0
+
+    lax.fori_loop(1, BLOCKS, finish_back, 0)
+    back_here = returned.at[:, pl.ds(0, SENT)]
+    pltpu.make_async_copy(back_here, back_here, return_sem.at[0]).wait()
+
+
+def place_rows(returned, pressure_out, spring_out):
+    planes = returned[:, 0:OWN].reshape(LANES, LANES).T
+    flat = pressure_out.reshape(CROSS * ROWS, LANES)
     for z in range(ROWS):
-        flat_out[pl.ds(z, CROSS, stride=ROWS), :] = final[z * CROSS:(z + 1) * CROSS]
-
-    pltpu.make_async_copy(spring_rows, spring_rows, row_sem.at[0]).wait()
+        flat[pl.ds(z, CROSS, stride=ROWS), :] = planes[z * CROSS:(z + 1) * CROSS]
+    owner = lax.broadcasted_iota(jnp.int32, (1, LANES), 1) // OWN
     total = jnp.zeros((1, LANES), F32)
     for d in range(BLOCKS):
-        total = jnp.where(lane[0:1] // OWN == d, spring_rows[d], total)
+        total = jnp.where(owner == d, returned[d, OWN:OWN + 1], total)
     spring_out[...] = total.reshape(spring_out.shape)
-
-    def finish_back(k, _):
-        planes, row = give_back(k)
-        planes.wait_send()
-        row.wait_send()
-        return 0
-
-    lax.fori_loop(1, BLOCKS, finish_back, 0)
 
 
 def lane_roll_by(x, shift):
@@ -437,20 +455,24 @@
 
 def on_device(pressure, layer, permeability, loading, spring, contact):
     vmem = pl.BlockSpec(memory_space=pltpu.VMEM)
-    smem = pl.BlockSpec(memory_space=pltpu.SMEM)
+    hbm = pl.BlockSpec(memory_space=pltpu.MemorySpace.HBM)
     planes = pltpu.VMEM((ROWS, GROUPS, CROSS, LANES), F32)
     plane = pltpu.VMEM((GROUPS, CROSS, LANES), F32)
     steps = pltpu.VMEM((4, GROUPS, CROSS, LANES), F32)
     tile = pltpu.VMEM((8, LANES), F32)
-    return pl.pallas_call(
+    returned = pl.pallas_call(
         kernel,
-        out_shape=(
-            jax.ShapeDtypeStruct(pressure.shape, F32),
-            jax.ShapeDtypeStruct(spring.shape, F32),
-        ),
-        in_specs=[smem, smem, vmem, vmem, vmem, vmem],
-        out_specs=(vmem, vmem),
+        out_shape=jax.ShapeDtypeStruct((BLOCKS, 2 * OWN, LANES), F32),
+        in_specs=[hbm] * 6,
+        out_specs=hbm,
         scratch_shapes=[
+            pltpu.SMEM(permeability.shape, F32),
+            pltpu.SMEM(contact.shape, jnp.int32),
+            pltpu.VMEM(pressure.shape, F32),
+            pltpu.VMEM(layer.shape, jnp.int32),
+            pltpu.VMEM(loading.shape, F32),
+            pltpu.VMEM(spring.shape, F32),
+            pltpu.SemaphoreType.DMA((6,)),
             pltpu.VMEM((3, LANES, LANES), F32),
             pltpu.VMEM((3, BLOCKS, WIDE, LANES), F32),
             pltpu.VMEM((BLOCKS, OWN, LANES), F32),
@@ -458,23 +480,27 @@
             planes, planes, planes, planes, planes, planes,
             planes, planes, planes, planes,
             steps, steps, plane, plane, plane, plane,
-            pltpu.VMEM((BLOCKS, OWN, LANES), F32),
-            pltpu.VMEM((BLOCKS, OWN, LANES), F32),
-            pltpu.VMEM((1, LANES), F32),
-            pltpu.VMEM((BLOCKS, 1, LANES), F32),
+            pltpu.VMEM((BLOCKS, 2 * OWN, LANES), F32),
             pltpu.SemaphoreType.DMA((3, BLOCKS + 1)),
             pltpu.SemaphoreType.DMA((3,)),
             pltpu.SemaphoreType.DMA((1,)),
             pltpu.SemaphoreType.DMA((2,)),
             pltpu.SemaphoreType.DMA((BLOCKS,)),
             pltpu.SemaphoreType.DMA((1,)),
-            pltpu.SemaphoreType.DMA((BLOCKS,)),
-            pltpu.SemaphoreType.DMA((1,)),
         ],
         compiler_params=pltpu.CompilerParams(
-            collective_id=0, has_side_effects=True, vmem_limit_bytes=24 << 20
+            collective_id=0, has_side_effects=True, vmem_limit_bytes=60 << 20
         ),
     )(permeability, contact, pressure, layer, loading, spring)
+    return pl.pallas_call(
+        place_rows,
+        out_shape=(
+            jax.ShapeDtypeStruct(pressure.shape, F32),
+            jax.ShapeDtypeStruct(spring.shape, F32),
+        ),
+        in_specs=[vmem],
+        out_specs=(vmem, vmem),
+    )(returned)
 
 
 def solution(mesh):

time: 34.3 us -> 28.1 us (0.82)
  local copies, waits for them, and re-layouts: 5.64 us -> 0 us
  Pallas kernels: 27.7 us -> 27.2 us
    unnamed x14 -> x0, local copies, waits for them, and re-layouts: 5.64 us -> none
    pallas_call x1 -> x2, Pallas kernels: 27.7 us -> 27.2 us  [the longest x1 25.6 us: on_device(): pl.pallas_call(kernel, out_shape=jax.ShapeDtypeStruct((BLOCKS, 2 * OWN, L...]
where the time goes in v2:
time: 28.1 us; the launch traced here: 27.9 us
  Pallas kernels  27.2 us (97%)
  between operations  0.64 us (2%)
    pallas_call x1, Pallas kernels, on_device(): pl.pallas_call(kernel, out_shape=jax.ShapeDtypeStruct((BLOCKS, 2 * OWN, L...  25.6 us
    pallas_call x1, Pallas kernels, on_device(): pl.pallas_call(place_rows, out_shape=(jax.ShapeDtypeStruct(pressure.shape...  1.64 us

profile of v2, /device:TPU:1, one launch (start us, length us, event | category | flops | bytes accessed | tf_op | source)
XLA Modules:
  0.0 27.9 jit_solution(6909842012451132646)
XLA Ops:
  0.6 25.6 %shard_map.77.returned = f32[16,16,128]{2,1,0:T(8,128)} custom-call(f32[2,8]{1,0:T(2,128)} %table_in.1, s32[8]{0:T(128)} %contact_in.1, f32[8,16,128]{2,1,0:T(8,128)} %pressure_in.1, s32[8,16,128]{2,1,0:T(8,128)} %layer_in.1, f32[8,16,128]{2,1,0:T(8,128)} %loading_in.1, f32[128]{0:T(128)} %spring_in.1), custom_call_target="tpu_custom_call" | custom-call | tf_op jit(solution)/shard_map/pallas_call | solution.py:463
  26.2 1.6 %shard_map.78 = (f32[8,16,128]{2,1,0:T(8,128)}, f32[128]{0:T(128)}) custom-call(f32[16,16,128]{2,1,0:T(8,128)} %shard_map.77.returned), custom_call_target="tpu_custom_call" | custom-call | tf_op jit(solution)/shard_map/pallas_call | solution.py:495

commit v3 on v2

--- a/solution.py
+++ b/solution.py
@@ -152,6 +152,9 @@
 
         lax.fori_loop(1, BLOCKS, deal, 0)
 
+    def for_each_side(which, act):
+        halo = HALO[which]
+
         @pl.when(has_right)
         def _():
             act(to_peer(which, (wall + 1, 0), LANES - halo, halo, OWN - halo, BLOCKS))
@@ -185,14 +188,15 @@
             no_column(which, halo, 2 * OWN).start()
 
     pack(LAYER, layer)
+    pack(PRESSURE, pressure)
+    pack(LOADING, loading)
     nothing[...] = jnp.zeros_like(nothing)
     sides = has_left.astype(jnp.int32) + has_right.astype(jnp.int32)
     pl.semaphore_wait(barrier, BLOCKS - 1 + sides)
-    deal_out(LAYER)
-    pack(PRESSURE, pressure)
-    deal_out(PRESSURE)
-    pack(LOADING, loading)
-    deal_out(LOADING)
+    for which in (LAYER, PRESSURE, LOADING):
+        for_each_side(which, lambda copy: copy.start())
+    for which in (LAYER, PRESSURE, LOADING):
+        deal_out(which)
 
     for copy in inputs[LOADING + 1:]:
         copy.wait()
@@ -418,6 +422,7 @@
     ).start()
 
     for which in (LAYER, PRESSURE, LOADING):
+        for_each_side(which, lambda copy: copy.wait_send())
         for_each_copy(which, lambda copy: copy.wait_send())
 
     @pl.when(first & has_right)

time: 28.1 us -> 26.7 us (0.950)
  the two profiles are of different devices: /device:TPU:1 before, /device:TPU:32 now
where the time goes in v3:
time: 26.7 us; the launch traced here: 26.6 us
  Pallas kernels  25.9 us (97%)
  between operations  0.64 us (2%)
    pallas_call x1, Pallas kernels, on_device(): pl.pallas_call(kernel, out_shape=jax.ShapeDtypeStruct((BLOCKS, 2 * OWN, L...  24.3 us
    pallas_call x1, Pallas kernels, on_device(): pl.pallas_call(place_rows, out_shape=(jax.ShapeDtypeStruct(pressure.shape...  1.64 us

profile of v3, /device:TPU:32, one launch (start us, length us, event | category | flops | bytes accessed | tf_op | source)
XLA Modules:
  0.0 26.6 jit_solution(2949289249851086974)
XLA Ops:
  0.6 24.3 %shard_map.77.returned = f32[16,16,128]{2,1,0:T(8,128)} custom-call(f32[2,8]{1,0:T(2,128)} %table_in.1, s32[8]{0:T(128)} %contact_in.1, f32[8,16,128]{2,1,0:T(8,128)} %pressure_in.1, s32[8,16,128]{2,1,0:T(8,128)} %layer_in.1, f32[8,16,128]{2,1,0:T(8,128)} %loading_in.1, f32[128]{0:T(128)} %spring_in.1), custom_call_target="tpu_custom_call" | custom-call | tf_op jit(solution)/shard_map/pallas_call | solution.py:468
  24.9 1.6 %shard_map.78 = (f32[8,16,128]{2,1,0:T(8,128)}, f32[128]{0:T(128)}) custom-call(f32[16,16,128]{2,1,0:T(8,128)} %shard_map.77.returned), custom_call_target="tpu_custom_call" | custom-call | tf_op jit(solution)/shard_map/pallas_call | solution.py:500

commit v4 on v3

--- a/solution.py
+++ b/solution.py
@@ -29,6 +29,12 @@
 MIDDLE = 7
 LAYER, PRESSURE, LOADING = 0, 1, 2
 HALO = (5, 6, 5)
+WIDTHS = tuple(OWN + 2 * halo for halo in HALO)
+SIDE = 4
+FAR_FIRST = sorted(
+    ((dy, dx) for dy in range(SIDE) for dx in range(SIDE) if dy or dx),
+    key=lambda at: -sum(min(step, SIDE - step) for step in at),
+)
 SENT = OWN + 1
 
 
@@ -55,11 +61,11 @@
     table_in, contact_in, pressure_in, layer_in, loading_in, spring_in,
     returned,
     table, contact, pressure, layer, loading, spring, in_sem,
-    packed, landed, nothing, wall_mine, wall_beside,
+    packed, landed, beyond, wall_mine, wall_beside,
     field, source, keep, along, back, ahead, chain, outward, from_prev, from_last,
     reduce_up, reduce_down, reduced_inv, sep_up, sep_down, springs,
     result,
-    send_sem, land_sem, wall_sem, wall_send, return_send, return_sem,
+    send_sem, land_sem, side_send, side_sem, wall_sem, wall_send, return_send, return_sem,
 ):
     wall, me = lax.axis_index("wall"), lax.axis_index("depth")
     walls = lax.axis_size("wall")
@@ -76,15 +82,13 @@
     for copy in inputs:
         copy.start()
 
+    peers = [
+        lax.rem(me // SIDE + dy, SIDE) * SIDE + lax.rem(me % SIDE + dx, SIDE) for dy, dx in FAR_FIRST
+    ]
+
     barrier = pltpu.get_barrier_semaphore()
-
-    def greet(k, _):
-        pl.semaphore_signal(
-            barrier, inc=1, device_id=(wall, lax.rem(me + k, BLOCKS)), device_id_type=MESH
-        )
-        return 0
-
-    lax.fori_loop(1, BLOCKS, greet, 0)
+    for peer in peers:
+        pl.semaphore_signal(barrier, inc=1, device_id=(wall, peer), device_id_type=MESH)
 
     @pl.when(first & has_left)
     def _():
@@ -106,97 +110,67 @@
         inputs[which].wait()
         flat = ref.reshape(CROSS * ROWS, LANES)
         planes = [flat[pl.ds(z, CROSS, stride=ROWS), :] for z in range(ROWS)]
-        packed[which] = jnp.concatenate(planes, 0).astype(F32).T
-
-    def to_peer(which, to, start, size, at, slot):
+        packed[which, OWN:OWN + LANES] = jnp.concatenate(planes, 0).astype(F32).T
+
+    def to_peer(which, peer):
+        width = OWN + 2 * HALO[which]
         return pltpu.make_async_remote_copy(
-            src_ref=packed.at[which, pl.ds(start, size)],
-            dst_ref=landed.at[which, me, pl.ds(at, size)],
-            send_sem=send_sem.at[which, slot],
-            recv_sem=land_sem.at[which],
-            device_id=to,
-            device_id_type=MESH,
+            src_ref=packed.at[which, pl.ds(peer * OWN + OWN - HALO[which], width)],
+            dst_ref=landed.at[which, me, pl.ds(OWN - HALO[which], width)],
+            send_sem=send_sem.at[0], recv_sem=land_sem.at[which],
+            device_id=(wall, peer), device_id_type=MESH,
         )
 
-    def to_self(which, start, size, at):
+    def to_self(which):
+        width = OWN + 2 * HALO[which]
         return pltpu.make_async_copy(
-            packed.at[which, pl.ds(start, size)],
-            landed.at[which, me, pl.ds(at, size)],
+            packed.at[which, pl.ds(me * OWN + OWN - HALO[which], width)],
+            landed.at[which, me, pl.ds(OWN - HALO[which], width)],
             land_sem.at[which],
         )
 
-    def no_column(which, size, at):
-        return pltpu.make_async_copy(
-            nothing.at[:, pl.ds(0, size)], landed.at[which, :, pl.ds(at, size)], land_sem.at[which]
+    def to_right(which):
+        return pltpu.make_async_remote_copy(
+            src_ref=packed.at[which, pl.ds(OWN + LANES - HALO[which], HALO[which])],
+            dst_ref=beyond.at[which, me, pl.ds(OWN - HALO[which], HALO[which])],
+            send_sem=side_send.at[0, which], recv_sem=side_sem.at[which],
+            device_id=(wall + 1, 0), device_id_type=MESH,
         )
 
-    def for_each_copy(which, act):
-        halo = HALO[which]
-
-        def deal(k, _):
-            to = lax.rem(me + k, BLOCKS)
-
-            @pl.when(to == 0)
-            def _():
-                act(to_peer(which, (wall, to), 0, OWN + halo, OWN, k))
-
-            @pl.when(to == BLOCKS - 1)
-            def _():
-                act(to_peer(which, (wall, to), LANES - OWN - halo, OWN + halo, OWN - halo, k))
-
-            @pl.when((to > 0) & (to < BLOCKS - 1))
-            def _():
-                act(to_peer(which, (wall, to), to * OWN - halo, OWN + 2 * halo, OWN - halo, k))
-
-            return 0
-
-        lax.fori_loop(1, BLOCKS, deal, 0)
-
-    def for_each_side(which, act):
-        halo = HALO[which]
-
-        @pl.when(has_right)
-        def _():
-            act(to_peer(which, (wall + 1, 0), LANES - halo, halo, OWN - halo, BLOCKS))
-
-        @pl.when(has_left)
-        def _():
-            act(to_peer(which, (wall - 1, BLOCKS - 1), 0, halo, 2 * OWN, 0))
-
-    def deal_out(which):
-        halo = HALO[which]
-        for_each_copy(which, lambda copy: copy.start())
-
-        @pl.when(first)
-        def _():
-            to_self(which, 0, OWN + halo, OWN).start()
-
-        @pl.when(last)
-        def _():
-            to_self(which, LANES - OWN - halo, OWN + halo, OWN - halo).start()
-
-        @pl.when(jnp.logical_not(first | last))
-        def _():
-            to_self(which, me * OWN - halo, OWN + 2 * halo, OWN - halo).start()
-
-        @pl.when(first & jnp.logical_not(has_left))
-        def _():
-            no_column(which, halo, OWN - halo).start()
-
-        @pl.when(last & jnp.logical_not(has_right))
-        def _():
-            no_column(which, halo, 2 * OWN).start()
-
+    def to_left(which):
+        return pltpu.make_async_remote_copy(
+            src_ref=packed.at[which, pl.ds(OWN, HALO[which])],
+            dst_ref=beyond.at[which, me, pl.ds(0, HALO[which])],
+            send_sem=side_send.at[1, which], recv_sem=side_sem.at[which],
+            device_id=(wall - 1, BLOCKS - 1), device_id_type=MESH,
+        )
+
+    for which in (LAYER, PRESSURE, LOADING):
+        packed[which, 0:OWN] = jnp.zeros((OWN, LANES), F32)
+        packed[which, OWN + LANES:] = jnp.zeros((OWN, LANES), F32)
     pack(LAYER, layer)
     pack(PRESSURE, pressure)
     pack(LOADING, loading)
-    nothing[...] = jnp.zeros_like(nothing)
     sides = has_left.astype(jnp.int32) + has_right.astype(jnp.int32)
     pl.semaphore_wait(barrier, BLOCKS - 1 + sides)
+
+    @pl.when(has_right)
+    def _():
+        for which in (LAYER, PRESSURE, LOADING):
+            to_right(which).start()
+
+    @pl.when(has_left)
+    def _():
+        for which in (LAYER, PRESSURE, LOADING):
+            to_left(which).start()
+
+    for peer in peers:
+        to_peer(LAYER, peer).start()
+    for peer in peers:
+        to_peer(PRESSURE, peer).start()
+        to_peer(LOADING, peer).start()
     for which in (LAYER, PRESSURE, LOADING):
-        for_each_side(which, lambda copy: copy.start())
-    for which in (LAYER, PRESSURE, LOADING):
-        deal_out(which)
+        to_self(which).start()
 
     for copy in inputs[LOADING + 1:]:
         copy.wait()
@@ -207,22 +181,22 @@
         share = jnp.where(lane // PANEL == panel, contact[panel].astype(F32), share)
     own_spring = jnp.broadcast_to(spring[...].reshape(1, LANES), (8, LANES))
     wall_mine[...] = jnp.where(sub == 0, own_spring, share)
-    to_right = pltpu.make_async_remote_copy(
+    wall_right = pltpu.make_async_remote_copy(
         src_ref=wall_mine, dst_ref=wall_beside, send_sem=wall_send.at[0], recv_sem=wall_sem.at[0],
         device_id=(wall + 1, 0), device_id_type=MESH,
     )
-    to_left = pltpu.make_async_remote_copy(
+    wall_left = pltpu.make_async_remote_copy(
         src_ref=wall_mine, dst_ref=wall_beside, send_sem=wall_send.at[1], recv_sem=wall_sem.at[0],
         device_id=(wall - 1, BLOCKS - 1), device_id_type=MESH,
     )
 
     @pl.when(first & has_right)
     def _():
-        to_right.start()
+        wall_right.start()
 
     @pl.when(last & has_left)
     def _():
-        to_left.start()
+        wall_left.start()
 
     wide = (GROUPS, CROSS, LANES)
     lanes = lax.broadcasted_iota(jnp.int32, wide, 2)
@@ -236,6 +210,20 @@
     def arrived(which):
         valid = landed.at[which, :, pl.ds(OWN - HALO[which], OWN + 2 * HALO[which])]
         pltpu.make_async_copy(valid, valid, land_sem.at[which]).wait()
+
+        @pl.when((first & has_left) | (last & has_right))
+        def _():
+            strip = beyond.at[which, :, pl.ds(0, HALO[which])]
+            pltpu.make_async_copy(strip, strip, side_sem.at[which]).wait()
+
+        @pl.when(first)
+        def _():
+            landed[which, :, 0:OWN] = jnp.where(has_left, beyond[which], 0.0)
+
+        @pl.when(last)
+        def _():
+            landed[which, :, 2 * OWN:] = jnp.where(has_right, beyond[which], 0.0)
+
         for g in range(GROUPS):
             rows = [landed[which, s, pl.ds(g, OWN, stride=GROUPS), :] for s in range(BLOCKS)]
             turned = jnp.concatenate(rows, 0).T.reshape(ROWS, CROSS, LANES)
@@ -404,40 +392,39 @@
     result[:, 0:OWN] = mine.T.reshape(BLOCKS, OWN, LANES)
     result[:, OWN:] = jnp.broadcast_to(own_columns(springs[...])[None], (BLOCKS, 8, LANES))
 
-    def give_back(k):
-        to = lax.rem(me + k, BLOCKS)
-        return pltpu.make_async_remote_copy(
-            src_ref=result.at[to, pl.ds(0, SENT)], dst_ref=returned.at[me, pl.ds(0, SENT)],
-            send_sem=return_send.at[k], recv_sem=return_sem.at[0],
-            device_id=(wall, to), device_id_type=MESH,
-        )
-
-    def start_back(k, _):
-        give_back(k).start()
-        return 0
-
-    lax.fori_loop(1, BLOCKS, start_back, 0)
+    for peer in peers:
+        pltpu.make_async_remote_copy(
+            src_ref=result.at[peer, pl.ds(0, SENT)], dst_ref=returned.at[me, pl.ds(0, SENT)],
+            send_sem=return_send.at[0], recv_sem=return_sem.at[0],
+            device_id=(wall, peer), device_id_type=MESH,
+        ).start()
     pltpu.make_async_copy(
         result.at[me, pl.ds(0, SENT)], returned.at[me, pl.ds(0, SENT)], return_sem.at[0]
     ).start()
 
-    for which in (LAYER, PRESSURE, LOADING):
-        for_each_side(which, lambda copy: copy.wait_send())
-        for_each_copy(which, lambda copy: copy.wait_send())
+    sent = landed.reshape(3 * BLOCKS * WIDE, LANES).at[pl.ds(0, (BLOCKS - 1) * sum(WIDTHS))]
+    pltpu.make_async_copy(sent, sent, send_sem.at[0]).wait()
+
+    @pl.when(has_right)
+    def _():
+        for which in (LAYER, PRESSURE, LOADING):
+            to_right(which).wait_send()
+
+    @pl.when(has_left)
+    def _():
+        for which in (LAYER, PRESSURE, LOADING):
+            to_left(which).wait_send()
 
     @pl.when(first & has_right)
     def _():
-        to_right.wait_send()
+        wall_right.wait_send()
 
     @pl.when(last & has_left)
     def _():
-        to_left.wait_send()
-
-    def finish_back(k, _):
-        give_back(k).wait_send()
-        return 0
-
-    lax.fori_loop(1, BLOCKS, finish_back, 0)
+        wall_left.wait_send()
+
+    given = result.at[pl.ds(0, BLOCKS - 1), pl.ds(0, SENT)]
+    pltpu.make_async_copy(given, given, return_send.at[0]).wait()
     back_here = returned.at[:, pl.ds(0, SENT)]
     pltpu.make_async_copy(back_here, back_here, return_sem.at[0]).wait()
 
@@ -478,19 +465,21 @@
             pltpu.VMEM(loading.shape, F32),
             pltpu.VMEM(spring.shape, F32),
             pltpu.SemaphoreType.DMA((6,)),
-            pltpu.VMEM((3, LANES, LANES), F32),
+            pltpu.VMEM((3, LANES + 2 * OWN, LANES), F32),
             pltpu.VMEM((3, BLOCKS, WIDE, LANES), F32),
-            pltpu.VMEM((BLOCKS, OWN, LANES), F32),
+            pltpu.VMEM((3, BLOCKS, OWN, LANES), F32),
             tile, tile,
             planes, planes, planes, planes, planes, planes,
             planes, planes, planes, planes,
             steps, steps, plane, plane, plane, plane,
             pltpu.VMEM((BLOCKS, 2 * OWN, LANES), F32),
-            pltpu.SemaphoreType.DMA((3, BLOCKS + 1)),
+            pltpu.SemaphoreType.DMA((1,)),
+            pltpu.SemaphoreType.DMA((3,)),
+            pltpu.SemaphoreType.DMA((2, 3)),
             pltpu.SemaphoreType.DMA((3,)),
             pltpu.SemaphoreType.DMA((1,)),
             pltpu.SemaphoreType.DMA((2,)),
-            pltpu.SemaphoreType.DMA((BLOCKS,)),
+            pltpu.SemaphoreType.DMA((1,)),
             pltpu.SemaphoreType.DMA((1,)),
         ],
         compiler_params=pltpu.CompilerParams(

time: 26.7 us -> 25.7 us (0.963)
  Pallas kernels: 25.9 us -> 24.9 us
    pallas_call x1, Pallas kernels: 24.3 us -> 23.3 us  [on_device(): pl.pallas_call(kernel, out_shape=jax.ShapeDtypeStruct((BLOCKS, 2 * OWN, L...]
where the time goes in v4:
time: 25.7 us; the launch traced here: 25.6 us
  Pallas kernels  24.9 us (97%)
  between operations  0.64 us (2%)
    pallas_call x1, Pallas kernels, on_device(): pl.pallas_call(kernel, out_shape=jax.ShapeDtypeStruct((BLOCKS, 2 * OWN, L...  23.3 us
    pallas_call x1, Pallas kernels, on_device(): pl.pallas_call(place_rows, out_shape=(jax.ShapeDtypeStruct(pressure.shape...  1.64 us

profile of v4, /device:TPU:32, one launch (start us, length us, event | category | flops | bytes accessed | tf_op | source)
XLA Modules:
  0.0 25.6 jit_solution(4217781557340089657)
XLA Ops:
  0.6 23.3 %shard_map.77.returned = f32[16,16,128]{2,1,0:T(8,128)} custom-call(f32[2,8]{1,0:T(2,128)} %table_in.1, s32[8]{0:T(128)} %contact_in.1, f32[8,16,128]{2,1,0:T(8,128)} %pressure_in.1, s32[8,16,128]{2,1,0:T(8,128)} %layer_in.1, f32[8,16,128]{2,1,0:T(8,128)} %loading_in.1, f32[128]{0:T(128)} %spring_in.1), custom_call_target="tpu_custom_call" | custom-call | tf_op jit(solution)/shard_map/pallas_call | solution.py:455
  23.9 1.6 %shard_map.78 = (f32[8,16,128]{2,1,0:T(8,128)}, f32[128]{0:T(128)}) custom-call(f32[16,16,128]{2,1,0:T(8,128)} %shard_map.77.returned), custom_call_target="tpu_custom_call" | custom-call | tf_op jit(solution)/shard_map/pallas_call | solution.py:489

commit v5 on v4

--- a/solution.py
+++ b/solution.py
@@ -63,7 +63,7 @@
     table, contact, pressure, layer, loading, spring, in_sem,
     packed, landed, beyond, wall_mine, wall_beside,
     field, source, keep, along, back, ahead, chain, outward, from_prev, from_last,
-    reduce_up, reduce_down, reduced_inv, sep_up, sep_down, springs,
+    last_end, last_start, prev_end, prev_start, sep_up, springs,
     result,
     send_sem, land_sem, side_send, side_sem, wall_sem, wall_send, return_send, return_sem,
 ):
@@ -151,27 +151,6 @@
     pack(LAYER, layer)
     pack(PRESSURE, pressure)
     pack(LOADING, loading)
-    sides = has_left.astype(jnp.int32) + has_right.astype(jnp.int32)
-    pl.semaphore_wait(barrier, BLOCKS - 1 + sides)
-
-    @pl.when(has_right)
-    def _():
-        for which in (LAYER, PRESSURE, LOADING):
-            to_right(which).start()
-
-    @pl.when(has_left)
-    def _():
-        for which in (LAYER, PRESSURE, LOADING):
-            to_left(which).start()
-
-    for peer in peers:
-        to_peer(LAYER, peer).start()
-    for peer in peers:
-        to_peer(PRESSURE, peer).start()
-        to_peer(LOADING, peer).start()
-    for which in (LAYER, PRESSURE, LOADING):
-        to_self(which).start()
-
     for copy in inputs[LOADING + 1:]:
         copy.wait()
     lane = lax.broadcasted_iota(jnp.int32, (8, LANES), 1)
@@ -190,6 +169,9 @@
         device_id=(wall - 1, BLOCKS - 1), device_id_type=MESH,
     )
 
+    sides = has_left.astype(jnp.int32) + has_right.astype(jnp.int32)
+    pl.semaphore_wait(barrier, BLOCKS - 1 + sides)
+
     @pl.when(first & has_right)
     def _():
         wall_right.start()
@@ -197,6 +179,24 @@
     @pl.when(last & has_left)
     def _():
         wall_left.start()
+
+    @pl.when(has_right)
+    def _():
+        for which in (LAYER, PRESSURE, LOADING):
+            to_right(which).start()
+
+    @pl.when(has_left)
+    def _():
+        for which in (LAYER, PRESSURE, LOADING):
+            to_left(which).start()
+
+    for peer in peers:
+        to_peer(LAYER, peer).start()
+    for peer in peers:
+        to_peer(PRESSURE, peer).start()
+        to_peer(LOADING, peer).start()
+    for which in (LAYER, PRESSURE, LOADING):
+        to_self(which).start()
 
     wide = (GROUPS, CROSS, LANES)
     lanes = lax.broadcasted_iota(jnp.int32, wide, 2)
@@ -282,16 +282,34 @@
     a_coef = up[LAST] * upper[LAST - 1]
     c_coef = down[LAST] * lane_roll(lower[0], -OWN)
     b_coef = diagonal[LAST] - up[LAST] * lower[LAST - 1] - down[LAST] * lane_roll(upper[0], -OWN)
-    sep_up[...], sep_down[...] = up[LAST], down[LAST]
+    sep_up[...] = up[LAST]
+    coefs = {0: jnp.ones(wide, F32)}
     for level in range(4):
-        hop = OWN << level
+        step = 1 << level
+        hop = OWN * step
         b_inv = 1.0 / b_coef
         alpha = a_coef * lane_roll(b_inv, hop)
         gamma = c_coef * lane_roll(b_inv, -hop)
-        reduce_up[level], reduce_down[level] = alpha, gamma
         b_coef = b_coef - alpha * lane_roll(c_coef, hop) - gamma * lane_roll(a_coef, -hop)
         a_coef, c_coef = alpha * lane_roll(a_coef, hop), gamma * lane_roll(c_coef, -hop)
-    reduced_inv[...] = 1.0 / b_coef
+        longer = dict(coefs)
+        for j, coef in coefs.items():
+            if 2 * step == BLOCKS:
+                moved = [((j + step) % BLOCKS, (alpha + gamma) * lane_roll(coef, hop))]
+            else:
+                moved = [
+                    ((j + step) % BLOCKS, alpha * lane_roll(coef, hop)),
+                    ((j - step) % BLOCKS, gamma * lane_roll(coef, -hop)),
+                ]
+            for at, term in moved:
+                longer[at] = longer[at] + term if at in longer else term
+        coefs = longer
+    b_inv = 1.0 / b_coef
+    for j in range(BLOCKS):
+        by_end = coefs[j] * b_inv
+        by_start = by_end * lane_roll(down[LAST], OWN * j)
+        last_end[j], last_start[(j - 1) % BLOCKS] = by_end, by_start
+        prev_end[(j + 1) % BLOCKS], prev_start[j] = lane_roll(by_end, OWN), lane_roll(by_start, OWN)
 
     @pl.when((first & has_left) | (last & has_right))
     def _():
@@ -348,18 +366,12 @@
             scaled[z] = scaled[z] + outward[z] * scaled[z + 1]
         for z in range(MIDDLE + 1, LAST):
             scaled[z] = scaled[z] + outward[z] * scaled[z - 1]
-        ends = (
-            scaled[LAST] + sep_up[...] * scaled[LAST - 1]
-            + sep_down[...] * lane_roll(scaled[0], -OWN)
-        )
-        for level in range(4):
-            hop = OWN << level
-            ends = (
-                ends + reduce_up[level] * lane_roll(ends, hop)
-                + reduce_down[level] * lane_roll(ends, -hop)
-            )
-        ends = ends * reduced_inv[...]
-        above = lane_roll(ends, OWN)
+        end, start = scaled[LAST] + sep_up[...] * scaled[LAST - 1], scaled[0]
+        ends, above = jnp.zeros(wide, F32), jnp.zeros(wide, F32)
+        for j in range(BLOCKS):
+            end_there, start_there = lane_roll(end, OWN * j), lane_roll(start, OWN * j)
+            ends = ends + last_end[j] * end_there + last_start[j] * start_there
+            above = above + prev_end[j] * end_there + prev_start[j] * start_there
         for z in range(LAST):
             field[z] = scaled[z] + from_prev[z] * above + from_last[z] * ends
         field[LAST] = ends
@@ -371,9 +383,15 @@
         moment = jnp.zeros(wide, F32)
         for z in range(ROWS):
             moment = moment + (base + float(z)) * field[z]
-        for level in range(4):
-            moment = moment + lane_roll(moment, OWN << level)
-        moment = moment * (1.0 / (ROWS * BLOCKS) ** 2)
+        row = lax.broadcasted_iota(jnp.int32, (CROSS, LANES), 0)
+        face = jnp.where(row == 0, moment[0], 0.0)
+        for g in range(1, GROUPS):
+            face = jnp.where(row == g, cross_roll(moment[g], g), face)
+        total = face
+        for j in range(1, BLOCKS):
+            total = total + lane_roll(face, OWN * j)
+        total = total * (1.0 / (ROWS * BLOCKS) ** 2)
+        moment = jnp.stack([cross_roll(total, -g) for g in range(GROUPS)])
         springs[...] = SPRING_KEEP * springs[...] + SPRING_DRIVE * touching * moment
         return carry
 
@@ -450,7 +468,6 @@
     hbm = pl.BlockSpec(memory_space=pltpu.MemorySpace.HBM)
     planes = pltpu.VMEM((ROWS, GROUPS, CROSS, LANES), F32)
     plane = pltpu.VMEM((GROUPS, CROSS, LANES), F32)
-    steps = pltpu.VMEM((4, GROUPS, CROSS, LANES), F32)
     tile = pltpu.VMEM((8, LANES), F32)
     returned = pl.pallas_call(
         kernel,
@@ -471,7 +488,7 @@
             tile, tile,
             planes, planes, planes, planes, planes, planes,
             planes, planes, planes, planes,
-            steps, steps, plane, plane, plane, plane,
+            planes, planes, planes, planes, plane, plane,
             pltpu.VMEM((BLOCKS, 2 * OWN, LANES), F32),
             pltpu.SemaphoreType.DMA((1,)),
             pltpu.SemaphoreType.DMA((3,)),

time: 25.7 us -> 23.7 us (0.922)
  Pallas kernels: 24.9 us -> 22.9 us
    pallas_call x1, Pallas kernels: 23.3 us -> 21.2 us  [on_device(): pl.pallas_call(kernel, out_shape=jax.ShapeDtypeStruct((BLOCKS, 2 * OWN, L...]
where the time goes in v5:
time: 23.7 us; the launch traced here: 23.5 us
  Pallas kernels  22.9 us (97%)
  between operations  0.64 us (3%)
    pallas_call x1, Pallas kernels, on_device(): pl.pallas_call(kernel, out_shape=jax.ShapeDtypeStruct((BLOCKS, 2 * OWN, L...  21.2 us
    pallas_call x1, Pallas kernels, on_device(): pl.pallas_call(place_rows, out_shape=(jax.ShapeDtypeStruct(pressure.shape...  1.64 us

profile of v5, /device:TPU:32, one launch (start us, length us, event | category | flops | bytes accessed | tf_op | source)
XLA Modules:
  0.0 23.5 jit_solution(7956535336692228383)
XLA Ops:
  0.6 21.2 %shard_map.77.returned = f32[16,16,128]{2,1,0:T(8,128)} custom-call(f32[2,8]{1,0:T(2,128)} %table_in.1, s32[8]{0:T(128)} %contact_in.1, f32[8,16,128]{2,1,0:T(8,128)} %pressure_in.1, s32[8,16,128]{2,1,0:T(8,128)} %layer_in.1, f32[8,16,128]{2,1,0:T(8,128)} %loading_in.1, f32[128]{0:T(128)} %spring_in.1), custom_call_target="tpu_custom_call" | custom-call | tf_op jit(solution)/shard_map/pallas_call | solution.py:472
  21.9 1.6 %shard_map.78 = (f32[8,16,128]{2,1,0:T(8,128)}, f32[128]{0:T(128)}) custom-call(f32[16,16,128]{2,1,0:T(8,128)} %shard_map.77.returned), custom_call_target="tpu_custom_call" | custom-call | tf_op jit(solution)/shard_map/pallas_call | solution.py:506

commit v6 on v5

v6 whole, which is shorter than its diff:
```python
import jax
import jax.numpy as jnp
from jax import lax
from jax.experimental import pallas as pl
from jax.experimental.pallas import tpu as pltpu
from jax.sharding import PartitionSpec as P

MESH = pl.DeviceIdType.MESH
F32 = jnp.float32

SOILS = 8
PANEL = 16
SUBSTEPS = 3
OUTER = 2
VNUM = 512.0
ALONG_RATE = 0.1
ACROSS_RATE = 0.06
SPRING_KEEP = 0.5
SPRING_DRIVE = 2.0

CROSS = 8
ROWS = 16
BLOCKS = 16
SOLVERS = 8
OWN = 16
MARGIN = 8
WIDE = OWN + 2 * MARGIN
SPOTS = 8
GROUPS = 4
LANES = 128
LAST = ROWS - 1
MIDDLE = 7
LAYER, PRESSURE, LOADING = 0, 1, 2
HALO = (5, 6, 5)
WIDTHS = tuple(OWN + 2 * halo for halo in HALO)
SIDE = 4
FAR_FIRST = sorted(
    ((dy, dx) for dy in range(SIDE) for dx in range(SIDE) if dy or dx),
    key=lambda at: -sum(min(step, SIDE - step) for step in at),
)
SENT = OWN + 1
ROOM = OWN + 8


def lane_roll(x, shift):
    return pltpu.roll(x, shift % LANES, x.ndim - 1)


def cross_roll(x, shift):
    return pltpu.roll(x, shift % CROSS, x.ndim - 2)


def harmonic(a, b):
    return (2.0 * VNUM) * a * b / (a + b)


def pick(level, table, row):
    value = jnp.full(level.shape, table[row, 0], F32)
    for soil in range(1, SOILS):
        value = jnp.where(level == float(soil), table[row, soil], value)
    return value


def kernel(
    table_in, contact_in, pressure_in, layer_in, loading_in, spring_in,
    returned,
    table, contact, pressure, layer, loading, spring, in_sem,
    packed, landed, beyond, wall_mine, wall_beside,
    field, source, keep, along, back, ahead, chain, outward, from_prev, from_last,
    last_end, last_start, prev_end, prev_start, sep_up, springs,
    turned, result,
    send_sem, land_sem, side_send, side_sem, wall_sem, wall_send, return_send, return_sem,
):
    wall, me = lax.axis_index("wall"), lax.axis_index("depth")
    walls = lax.axis_size("wall")
    has_left, has_right = wall > 0, wall < walls - 1

    def shift_of(wall):
        return SOLVERS * lax.rem(wall, 2)

    def spot_of(device):
        return lax.rem(device + BLOCKS - shift_of(wall), BLOCKS)

    mine = spot_of(me)
    solves, first, last = mine < SOLVERS, mine == 0, mine == SOLVERS - 1
    left_end = (wall - 1, shift_of(wall + 1) + SOLVERS - 1)
    right_end = (wall + 1, shift_of(wall + 1))

    inputs = [
        pltpu.make_async_copy(source_ref, here, in_sem.at[at])
        for at, (source_ref, here) in enumerate((
            (layer_in, layer), (pressure_in, pressure), (loading_in, loading),
            (spring_in, spring), (contact_in, contact), (table_in, table),
        ))
    ]
    for copy in inputs:
        copy.start()

    peers = [
        lax.rem(me // SIDE + dy, SIDE) * SIDE + lax.rem(me % SIDE + dx, SIDE) for dy, dx in FAR_FIRST
    ]

    barrier = pltpu.get_barrier_semaphore()

    @pl.when(solves)
    def _():
        for peer in peers:
            pl.semaphore_signal(barrier, inc=1, device_id=(wall, peer), device_id_type=MESH)

    @pl.when(first & has_left)
    def _():
        def call(k, _):
            pl.semaphore_signal(barrier, inc=1, device_id=(wall - 1, k), device_id_type=MESH)
            return 0

        lax.fori_loop(0, BLOCKS, call, 0)

    @pl.when(last & has_right)
    def _():
        def call(k, _):
            pl.semaphore_signal(barrier, inc=1, device_id=(wall + 1, k), device_id_type=MESH)
            return 0

        lax.fori_loop(0, BLOCKS, call, 0)

    def pack(which, ref):
        inputs[which].wait()
        flat = ref.reshape(CROSS * ROWS, LANES)
        planes = [flat[pl.ds(z, CROSS, stride=ROWS), :] for z in range(ROWS)]
        packed[which, MARGIN:MARGIN + LANES] = jnp.concatenate(planes, 0).astype(F32).T

    def to_peer(which, peer):
        width = OWN + 2 * HALO[which]
        return pltpu.make_async_remote_copy(
            src_ref=packed.at[which, pl.ds(spot_of(peer) * OWN + MARGIN - HALO[which], width)],
            dst_ref=landed.at[which, me, pl.ds(MARGIN - HALO[which], width)],
            send_sem=send_sem.at[0], recv_sem=land_sem.at[which],
            device_id=(wall, peer), device_id_type=MESH,
        )

    def to_self(which):
        width = OWN + 2 * HALO[which]
        return pltpu.make_async_copy(
            packed.at[which, pl.ds(mine * OWN + MARGIN - HALO[which], width)],
            landed.at[which, me, pl.ds(MARGIN - HALO[which], width)],
            land_sem.at[which],
        )

    def to_right(which):
        return pltpu.make_async_remote_copy(
            src_ref=packed.at[which, pl.ds(MARGIN + LANES - HALO[which], HALO[which])],
            dst_ref=beyond.at[which, me, pl.ds(MARGIN - HALO[which], HALO[which])],
            send_sem=side_send.at[0, which], recv_sem=side_sem.at[which],
            device_id=right_end, device_id_type=MESH,
        )

    def to_left(which):
        return pltpu.make_async_remote_copy(
            src_ref=packed.at[which, pl.ds(MARGIN, HALO[which])],
            dst_ref=beyond.at[which, me, pl.ds(0, HALO[which])],
            send_sem=side_send.at[1, which], recv_sem=side_sem.at[which],
            device_id=left_end, device_id_type=MESH,
        )

    for which in (LAYER, PRESSURE, LOADING):
        packed[which, 0:MARGIN] = jnp.zeros((MARGIN, LANES), F32)
        packed[which, MARGIN + LANES:] = jnp.zeros((MARGIN, LANES), F32)
    pack(LAYER, layer)
    pack(PRESSURE, pressure)
    pack(LOADING, loading)
    for copy in inputs[LOADING + 1:]:
        copy.wait()
    lane = lax.broadcasted_iota(jnp.int32, (8, LANES), 1)
    sub = lax.broadcasted_iota(jnp.int32, (8, LANES), 0)
    share = jnp.zeros((8, LANES), F32)
    for panel in range(LANES // PANEL):
        share = jnp.where(lane // PANEL == panel, contact[panel].astype(F32), share)
    own_spring = jnp.broadcast_to(spring[...].reshape(1, LANES), (8, LANES))
    wall_mine[...] = jnp.where(sub == 0, own_spring, share)
    wall_right = pltpu.make_async_remote_copy(
        src_ref=wall_mine, dst_ref=wall_beside, send_sem=wall_send.at[0], recv_sem=wall_sem.at[0],
        device_id=right_end, device_id_type=MESH,
    )
    wall_left = pltpu.make_async_remote_copy(
        src_ref=wall_mine, dst_ref=wall_beside, send_sem=wall_send.at[1], recv_sem=wall_sem.at[0],
        device_id=left_end, device_id_type=MESH,
    )

    sides = has_left.astype(jnp.int32) + has_right.astype(jnp.int32)
    pl.semaphore_wait(barrier, SOLVERS - solves.astype(jnp.int32) + sides)

    @pl.when(first & has_right)
    def _():
        wall_right.start()

    @pl.when(last & has_left)
    def _():
        wall_left.start()

    @pl.when(has_right)
    def _():
        for which in (LAYER, PRESSURE, LOADING):
            to_right(which).start()

    @pl.when(has_left)
    def _():
        for which in (LAYER, PRESSURE, LOADING):
            to_left(which).start()

    def deal(peer, *arrays):
        @pl.when(spot_of(peer) < SOLVERS)
        def _():
            for which in arrays:
                to_peer(which, peer).start()

    for peer in peers:
        deal(peer, LAYER)
    for peer in peers:
        deal(peer, PRESSURE, LOADING)

    @pl.when(solves)
    def _():
        for which in (LAYER, PRESSURE, LOADING):
            to_self(which).start()

    @pl.when(solves)
    def _():
        wide = (GROUPS, CROSS, LANES)
        lanes = lax.broadcasted_iota(jnp.int32, wide, 2)
        block = lanes // SPOTS
        column = GROUPS * (lanes % SPOTS) + lax.broadcasted_iota(jnp.int32, wide, 0)
        cross = lax.broadcasted_iota(jnp.int32, wide, 1)
        place = wall * LANES + mine * OWN - MARGIN + column
        inside = (place >= 0) & (place < walls * LANES)
        top, bottom = block == 0, block == BLOCKS - 1

        def arrived(which):
            valid = landed.at[which, :, pl.ds(MARGIN - HALO[which], OWN + 2 * HALO[which])]
            pltpu.make_async_copy(valid, valid, land_sem.at[which]).wait()

            @pl.when((first & has_left) | (last & has_right))
            def _():
                strip = beyond.at[which, :, pl.ds(0, HALO[which])]
                pltpu.make_async_copy(strip, strip, side_sem.at[which]).wait()

            @pl.when(first)
            def _():
                landed[which, :, 0:MARGIN] = jnp.where(has_left, beyond[which], 0.0)

            @pl.when(last)
            def _():
                landed[which, :, OWN + MARGIN:] = jnp.where(has_right, beyond[which], 0.0)

            for g in range(GROUPS):
                rows = [landed[which, s, pl.ds(g, SPOTS, stride=GROUPS), :] for s in range(BLOCKS)]
                planes = jnp.concatenate(rows, 0).T.reshape(ROWS, CROSS, LANES)
                field_or = source if which == LOADING else field
                field_or[:, g] = planes

        arrived(LAYER)
        perm = [pick(field[z], table, 0) for z in range(ROWS)]
        up = [None] * ROWS
        for z in range(1, ROWS):
            up[z] = harmonic(perm[z - 1], perm[z])
        up[0] = jnp.where(top, VNUM * perm[0], harmonic(lane_roll(perm[LAST], SPOTS), perm[0]))
        down = up[1:] + [jnp.where(bottom, 0.0, lane_roll(up[0], -SPOTS))]
        diagonal = [1.0 + up[z] + down[z] for z in range(ROWS)]

        inverse, toward = [None] * ROWS, [None] * ROWS
        chained = [None] * ROWS
        for z in range(MIDDLE):
            pivot = diagonal[z] if z == 0 else diagonal[z] - up[z] * toward[z - 1]
            inverse[z] = 1.0 / pivot
            toward[z] = down[z] * inverse[z]
            chained[z] = up[z] * inverse[z]
        for z in range(LAST - 1, MIDDLE, -1):
            pivot = diagonal[z] if z == LAST - 1 else diagonal[z] - down[z] * toward[z + 1]
            inverse[z] = 1.0 / pivot
            toward[z] = up[z] * inverse[z]
            chained[z] = down[z] * inverse[z]
        inverse[MIDDLE] = 1.0 / (
            diagonal[MIDDLE] - up[MIDDLE] * toward[MIDDLE - 1] - down[MIDDLE] * toward[MIDDLE + 1]
        )
        chained[MIDDLE] = up[MIDDLE] * inverse[MIDDLE]
        toward[MIDDLE] = down[MIDDLE] * inverse[MIDDLE]
        inverse[LAST] = jnp.ones(wide, F32)

        upper, lower = [None] * LAST, [None] * LAST
        upper[0] = jnp.where(top, 0.0, chained[0])
        for z in range(1, MIDDLE):
            upper[z] = chained[z] * upper[z - 1]
        upper[MIDDLE] = chained[MIDDLE] * upper[MIDDLE - 1]
        for z in range(MIDDLE - 1, -1, -1):
            upper[z] = upper[z] + toward[z] * upper[z + 1]
        for z in range(MIDDLE + 1, LAST):
            upper[z] = toward[z] * upper[z - 1]
        lower[LAST - 1] = chained[LAST - 1]
        for z in range(LAST - 2, MIDDLE, -1):
            lower[z] = chained[z] * lower[z + 1]
        lower[MIDDLE] = toward[MIDDLE] * lower[MIDDLE + 1]
        for z in range(MIDDLE + 1, LAST):
            lower[z] = lower[z] + toward[z] * lower[z - 1]
        for z in range(MIDDLE - 1, -1, -1):
            lower[z] = toward[z] * lower[z + 1]
        for z in range(LAST):
            chain[z], outward[z] = chained[z], toward[z]
            from_prev[z], from_last[z] = upper[z], lower[z]

        a_coef = up[LAST] * upper[LAST - 1]
        c_coef = down[LAST] * lane_roll(lower[0], -SPOTS)
        b_coef = diagonal[LAST] - up[LAST] * lower[LAST - 1] - down[LAST] * lane_roll(upper[0], -SPOTS)
        sep_up[...] = up[LAST]
        coefs = {0: jnp.ones(wide, F32)}
        for level in range(4):
            step = 1 << level
            hop = SPOTS * step
            b_inv = 1.0 / b_coef
            alpha = a_coef * lane_roll(b_inv, hop)
            gamma = c_coef * lane_roll(b_inv, -hop)
            b_coef = b_coef - alpha * lane_roll(c_coef, hop) - gamma * lane_roll(a_coef, -hop)
            a_coef, c_coef = alpha * lane_roll(a_coef, hop), gamma * lane_roll(c_coef, -hop)
            longer = dict(coefs)
            for j, coef in coefs.items():
                if 2 * step == BLOCKS:
                    moved = [((j + step) % BLOCKS, (alpha + gamma) * lane_roll(coef, hop))]
                else:
                    moved = [
                        ((j + step) % BLOCKS, alpha * lane_roll(coef, hop)),
                        ((j - step) % BLOCKS, gamma * lane_roll(coef, -hop)),
                    ]
                for at, term in moved:
                    longer[at] = longer[at] + term if at in longer else term
            coefs = longer
        b_inv = 1.0 / b_coef
        for j in range(BLOCKS):
            by_end = coefs[j] * b_inv
            by_start = by_end * lane_roll(down[LAST], SPOTS * j)
            last_end[j], last_start[(j - 1) % BLOCKS] = by_end, by_start
            prev_end[(j + 1) % BLOCKS], prev_start[j] = lane_roll(by_end, SPOTS), lane_roll(by_start, SPOTS)

        @pl.when((first & has_left) | (last & has_right))
        def _():
            pltpu.make_async_copy(wall_beside, wall_beside, wall_sem.at[0]).wait()

        @pl.when(jnp.logical_not((first & has_left) | (last & has_right)))
        def _():
            wall_beside[...] = jnp.zeros_like(wall_beside)

        beside = (first & (lane >= LANES - MARGIN)) | (last & (lane < MARGIN))
        window = jnp.where(beside, wall_beside[...], wall_mine[...])
        window = lane_roll_by(window, lax.rem(2 * LANES + MARGIN - mine * OWN, LANES))
        touching = []
        for g in range(GROUPS):
            spread = jnp.take_along_axis(window, GROUPS * (lane % SPOTS) + g, axis=1)
            springs[g] = jnp.broadcast_to(spread[0:1], (CROSS, LANES))
            touching.append(jnp.broadcast_to(spread[1:2], (CROSS, LANES)))
        touching = jnp.stack(touching)

        ahead_mask = (cross < CROSS - 1).astype(F32)
        back_mask = jnp.where(cross > 0, 1.0, touching)
        for z in range(ROWS):
            lateral = jnp.where(inside, pick(field[z], table, 1), 0.0)
            a1 = ALONG_RATE * lateral
            a2 = ACROSS_RATE * lateral
            a2b, a2a = a2 * back_mask, a2 * ahead_mask
            keep[z] = (1.0 - 2.0 * a1 - a2b - a2a) * inverse[z]
            along[z], back[z], ahead[z] = a1 * inverse[z], a2b * inverse[z], a2a * inverse[z]
        arrived(LOADING)
        for z in range(ROWS):
            source[z] = source[z] * inverse[z]
        arrived(PRESSURE)

        def solve(_, carry):
            spring_now = springs[...]
            scaled = []
            for z in range(ROWS):
                now = field[z]
                left = jnp.stack([lane_roll(now[3], 1), now[0], now[1], now[2]])
                right = jnp.stack([now[1], now[2], now[3], lane_roll(now[0], -1)])
                behind = jnp.where(cross == 0, spring_now, cross_roll(now, 1))
                scaled.append(
                    source[z] + keep[z] * now + along[z] * (left + right)
                    + back[z] * behind + ahead[z] * cross_roll(now, -1)
                )
            for z in range(1, MIDDLE):
                scaled[z] = scaled[z] + chain[z] * scaled[z - 1]
            for z in range(LAST - 2, MIDDLE, -1):
                scaled[z] = scaled[z] + chain[z] * scaled[z + 1]
            scaled[MIDDLE] = (
                scaled[MIDDLE] + chain[MIDDLE] * scaled[MIDDLE - 1] + outward[MIDDLE] * scaled[MIDDLE + 1]
            )
            for z in range(MIDDLE - 1, -1, -1):
                scaled[z] = scaled[z] + outward[z] * scaled[z + 1]
            for z in range(MIDDLE + 1, LAST):
                scaled[z] = scaled[z] + outward[z] * scaled[z - 1]
            end, start = scaled[LAST] + sep_up[...] * scaled[LAST - 1], scaled[0]
            ends, above = jnp.zeros(wide, F32), jnp.zeros(wide, F32)
            for j in range(BLOCKS):
                end_there, start_there = lane_roll(end, SPOTS * j), lane_roll(start, SPOTS * j)
                ends = ends + last_end[j] * end_there + last_start[j] * start_there
                above = above + prev_end[j] * end_there + prev_start[j] * start_there
            for z in range(LAST):
                field[z] = scaled[z] + from_prev[z] * above + from_last[z] * ends
            field[LAST] = ends
            return carry

        def outer_step(_, carry):
            lax.fori_loop(0, SUBSTEPS, solve, 0)
            base = ROWS * block.astype(F32) + 0.5
            moment = jnp.zeros(wide, F32)
            for z in range(ROWS):
                moment = moment + (base + float(z)) * field[z]
            row = lax.broadcasted_iota(jnp.int32, (CROSS, LANES), 0)
            face = jnp.where(row == 0, moment[0], 0.0)
            for g in range(1, GROUPS):
                face = jnp.where(row == g, cross_roll(moment[g], g), face)
            total = face
            for j in range(1, BLOCKS):
                total = total + lane_roll(face, SPOTS * j)
            total = total * (1.0 / (ROWS * BLOCKS) ** 2)
            moment = jnp.stack([cross_roll(total, -g) for g in range(GROUPS)])
            springs[...] = SPRING_KEEP * springs[...] + SPRING_DRIVE * touching * moment
            return carry

        lax.fori_loop(0, OUTER, outer_step, 0)

        for g in range(GROUPS):
            turned[g] = field[:, g].reshape(LANES, LANES).T
        flat_result = result.reshape(BLOCKS * ROOM, LANES)
        for at in range(OWN):
            i, g = divmod(MARGIN + at, GROUPS)
            for half in range(2):
                flat_result[pl.ds(at + half * 8 * ROOM, 8, stride=ROOM), :] = (
                    turned[g, pl.ds(i + half * 8 * SPOTS, 8, stride=SPOTS), :]
                )
        spring_row = jnp.zeros((8, LANES), F32)
        for g in range(GROUPS):
            spread = jnp.take_along_axis(
                springs[g], (MARGIN + lane % OWN) // GROUPS, axis=1
            )
            spring_row = jnp.where(lane % GROUPS == g, spread, spring_row)
        result[:, OWN:] = jnp.broadcast_to(spring_row[None], (BLOCKS, 8, LANES))

        for peer in peers:
            pltpu.make_async_remote_copy(
                src_ref=result.at[peer, pl.ds(0, SENT)], dst_ref=returned.at[mine, pl.ds(0, SENT)],
                send_sem=return_send.at[0], recv_sem=return_sem.at[0],
                device_id=(wall, peer), device_id_type=MESH,
            ).start()
        pltpu.make_async_copy(
            result.at[me, pl.ds(0, SENT)], returned.at[mine, pl.ds(0, SENT)], return_sem.at[0]
        ).start()

    def wait_dealt(count):
        sent = landed.reshape(3 * BLOCKS * WIDE, LANES).at[pl.ds(0, count * sum(WIDTHS))]
        pltpu.make_async_copy(sent, sent, send_sem.at[0]).wait()

    @pl.when(solves)
    def _():
        wait_dealt(SOLVERS - 1)

    @pl.when(jnp.logical_not(solves))
    def _():
        wait_dealt(SOLVERS)

    @pl.when(has_right)
    def _():
        for which in (LAYER, PRESSURE, LOADING):
            to_right(which).wait_send()

    @pl.when(has_left)
    def _():
        for which in (LAYER, PRESSURE, LOADING):
            to_left(which).wait_send()

    @pl.when(first & has_right)
    def _():
        wall_right.wait_send()

    @pl.when(last & has_left)
    def _():
        wall_left.wait_send()

    @pl.when(solves)
    def _():
        given = result.reshape(BLOCKS * ROOM, LANES).at[pl.ds(0, (BLOCKS - 1) * SENT)]
        pltpu.make_async_copy(given, given, return_send.at[0]).wait()

    back_here = returned.at[:, pl.ds(0, SENT)]
    pltpu.make_async_copy(back_here, back_here, return_sem.at[0]).wait()


def place_rows(returned, pressure_out, spring_out):
    planes = returned[:, 0:OWN].reshape(LANES, LANES).T
    flat = pressure_out.reshape(CROSS * ROWS, LANES)
    for z in range(ROWS):
        flat[pl.ds(z, CROSS, stride=ROWS), :] = planes[z * CROSS:(z + 1) * CROSS]
    owner = lax.broadcasted_iota(jnp.int32, (1, LANES), 1) // OWN
    total = jnp.zeros((1, LANES), F32)
    for d in range(SOLVERS):
        total = jnp.where(owner == d, returned[d, OWN:OWN + 1], total)
    spring_out[...] = total.reshape(spring_out.shape)


def lane_roll_by(x, shift):
    return pltpu.roll(x, shift, x.ndim - 1)


def on_device(pressure, layer, permeability, loading, spring, contact):
    vmem = pl.BlockSpec(memory_space=pltpu.VMEM)
    hbm = pl.BlockSpec(memory_space=pltpu.MemorySpace.HBM)
    planes = pltpu.VMEM((ROWS, GROUPS, CROSS, LANES), F32)
    plane = pltpu.VMEM((GROUPS, CROSS, LANES), F32)
    tile = pltpu.VMEM((8, LANES), F32)
    returned = pl.pallas_call(
        kernel,
        out_shape=jax.ShapeDtypeStruct((SOLVERS, ROOM, LANES), F32),
        in_specs=[hbm] * 6,
        out_specs=hbm,
        scratch_shapes=[
            pltpu.SMEM(permeability.shape, F32),
            pltpu.SMEM(contact.shape, jnp.int32),
            pltpu.VMEM(pressure.shape, F32),
            pltpu.VMEM(layer.shape, jnp.int32),
            pltpu.VMEM(loading.shape, F32),
            pltpu.VMEM(spring.shape, F32),
            pltpu.SemaphoreType.DMA((6,)),
            pltpu.VMEM((3, LANES + 2 * MARGIN, LANES), F32),
            pltpu.VMEM((3, BLOCKS, WIDE, LANES), F32),
            pltpu.VMEM((3, BLOCKS, MARGIN, LANES), F32),
            tile, tile,
            planes, planes, planes, planes, planes, planes,
            planes, planes, planes, planes,
            planes, planes, planes, planes, plane, plane,
            pltpu.VMEM((GROUPS, LANES, LANES), F32),
            pltpu.VMEM((BLOCKS, ROOM, LANES), F32),
            pltpu.SemaphoreType.DMA((1,)),
            pltpu.SemaphoreType.DMA((3,)),
            pltpu.SemaphoreType.DMA((2, 3)),
            pltpu.SemaphoreType.DMA((3,)),
            pltpu.SemaphoreType.DMA((1,)),
            pltpu.SemaphoreType.DMA((2,)),
            pltpu.SemaphoreType.DMA((1,)),
            pltpu.SemaphoreType.DMA((1,)),
        ],
        compiler_params=pltpu.CompilerParams(
            collective_id=0, has_side_effects=True, vmem_limit_bytes=60 << 20
        ),
    )(permeability, contact, pressure, layer, loading, spring)
    return pl.pallas_call(
        place_rows,
        out_shape=(
            jax.ShapeDtypeStruct(pressure.shape, F32),
            jax.ShapeDtypeStruct(spring.shape, F32),
        ),
        in_specs=[vmem],
        out_specs=(vmem, vmem),
    )(returned)


def solution(mesh):
    cells = P(None, "depth", "wall")
    return jax.shard_map(
        on_device,
        mesh=mesh,
        in_specs=(cells, cells, P(), cells, P("wall"), P("wall")),
        out_specs=(cells, P("wall")),
        check_vma=False,
    )
```

time: 23.7 us -> 22.6 us (0.954)
  the two profiles are of different devices: /device:TPU:32 before, /device:TPU:1 now
where the time goes in v6:
time: 22.6 us; the launch traced here: 22.3 us
  Pallas kernels  21.6 us (96%)
  between operations  0.64 us (3%)
    pallas_call x1, Pallas kernels, on_device(): pl.pallas_call(kernel, out_shape=jax.ShapeDtypeStruct((SOLVERS, ROOM, LAN...  20 us
    pallas_call x1, Pallas kernels, on_device(): pl.pallas_call(place_rows, out_shape=(jax.ShapeDtypeStruct(pressure.shape...  1.63 us

profile of v6, /device:TPU:1, one launch (start us, length us, event | category | flops | bytes accessed | tf_op | source)
XLA Modules:
  0.0 22.3 jit_solution(14779956018727741868)
XLA Ops:
  0.6 20.0 %shard_map.77.returned = f32[8,24,128]{2,1,0:T(8,128)} custom-call(f32[2,8]{1,0:T(2,128)} %table_in.1, s32[8]{0:T(128)} %contact_in.1, f32[8,16,128]{2,1,0:T(8,128)} %pressure_in.1, s32[8,16,128]{2,1,0:T(8,128)} %layer_in.1, f32[8,16,128]{2,1,0:T(8,128)} %loading_in.1, f32[128]{0:T(128)} %spring_in.1), custom_call_target="tpu_custom_call" | custom-call | tf_op jit(solution)/shard_map/pallas_call | solution.py:515
  20.6 1.6 %shard_map.78 = (f32[8,16,128]{2,1,0:T(8,128)}, f32[128]{0:T(128)}) custom-call(f32[8,24,128]{2,1,0:T(8,128)} %shard_map.77.returned), custom_call_target="tpu_custom_call" | custom-call | tf_op jit(solution)/shard_map/pallas_call | solution.py:550

commit v7 on v6

--- a/solution.py
+++ b/solution.py
@@ -22,6 +22,7 @@
 ROWS = 16
 BLOCKS = 16
 SOLVERS = 8
+MOVED = 5
 OWN = 16
 MARGIN = 8
 WIDE = OWN + 2 * MARGIN
@@ -79,12 +80,13 @@
         return SOLVERS * lax.rem(wall, 2)
 
     def spot_of(device):
-        return lax.rem(device + BLOCKS - shift_of(wall), BLOCKS)
+        at = lax.rem(device + BLOCKS - shift_of(wall), BLOCKS)
+        return jnp.where(at < SOLVERS, lax.rem(at + SOLVERS - MOVED, SOLVERS), at)
 
     mine = spot_of(me)
     solves, first, last = mine < SOLVERS, mine == 0, mine == SOLVERS - 1
-    left_end = (wall - 1, shift_of(wall + 1) + SOLVERS - 1)
-    right_end = (wall + 1, shift_of(wall + 1))
+    left_end = (wall - 1, shift_of(wall + 1) + (SOLVERS - 1 + MOVED) % SOLVERS)
+    right_end = (wall + 1, shift_of(wall + 1) + MOVED)
 
     inputs = [
         pltpu.make_async_copy(source_ref, here, in_sem.at[at])

time: 22.6 us -> 22.3 us (0.987)
  no operation moved by 1% of the time
where the time goes in v7:
time: 22.3 us; the launch traced here: 22.1 us
  Pallas kernels  21.4 us (96%)
  between operations  0.64 us (3%)
    pallas_call x1, Pallas kernels, on_device(): pl.pallas_call(kernel, out_shape=jax.ShapeDtypeStruct((SOLVERS, ROOM, LAN...  19.8 us
    pallas_call x1, Pallas kernels, on_device(): pl.pallas_call(place_rows, out_shape=(jax.ShapeDtypeStruct(pressure.shape...  1.63 us

profile of v7, /device:TPU:1, one launch (start us, length us, event | category | flops | bytes accessed | tf_op | source)
XLA Modules:
  0.0 22.1 jit_solution(5425779582129714784)
XLA Ops:
  0.6 19.8 %shard_map.77.returned = f32[8,24,128]{2,1,0:T(8,128)} custom-call(f32[2,8]{1,0:T(2,128)} %table_in.1, s32[8]{0:T(128)} %contact_in.1, f32[8,16,128]{2,1,0:T(8,128)} %pressure_in.1, s32[8,16,128]{2,1,0:T(8,128)} %layer_in.1, f32[8,16,128]{2,1,0:T(8,128)} %loading_in.1, f32[128]{0:T(128)} %spring_in.1), custom_call_target="tpu_custom_call" | custom-call | tf_op jit(solution)/shard_map/pallas_call | solution.py:517
  20.5 1.6 %shard_map.78 = (f32[8,16,128]{2,1,0:T(8,128)}, f32[128]{0:T(128)}) custom-call(f32[8,24,128]{2,1,0:T(8,128)} %shard_map.77.returned), custom_call_target="tpu_custom_call" | custom-call | tf_op jit(solution)/shard_map/pallas_call | solution.py:552

commit v8 on v7

--- a/solution.py
+++ b/solution.py
@@ -1,3 +1,5 @@
+import functools
+
 import jax
 import jax.numpy as jnp
 from jax import lax
@@ -22,7 +24,7 @@
 ROWS = 16
 BLOCKS = 16
 SOLVERS = 8
-MOVED = 5
+MOVED = 1
 OWN = 16
 MARGIN = 8
 WIDE = OWN + 2 * MARGIN
@@ -39,6 +41,7 @@
     ((dy, dx) for dy in range(SIDE) for dx in range(SIDE) if dy or dx),
     key=lambda at: -sum(min(step, SIDE - step) for step in at),
 )
+EARLY_FIRST = sorted(range(BLOCKS), key=lambda device: device // SIDE + device % SIDE)
 SENT = OWN + 1
 ROOM = OWN + 8
 
@@ -407,7 +410,7 @@
             return carry
 
         def outer_step(_, carry):
-            lax.fori_loop(0, SUBSTEPS, solve, 0)
+            lax.fori_loop(0, SUBSTEPS, solve, 0, unroll=True)
             base = ROWS * block.astype(F32) + 0.5
             moment = jnp.zeros(wide, F32)
             for z in range(ROWS):
@@ -424,7 +427,8 @@
             springs[...] = SPRING_KEEP * springs[...] + SPRING_DRIVE * touching * moment
             return carry
 
-        lax.fori_loop(0, OUTER, outer_step, 0)
+        for step in range(OUTER):
+            outer_step(step, 0)
 
         for g in range(GROUPS):
             turned[g] = field[:, g].reshape(LANES, LANES).T
@@ -443,12 +447,15 @@
             spring_row = jnp.where(lane % GROUPS == g, spread, spring_row)
         result[:, OWN:] = jnp.broadcast_to(spring_row[None], (BLOCKS, 8, LANES))
 
-        for peer in peers:
+        def give_back(device):
             pltpu.make_async_remote_copy(
-                src_ref=result.at[peer, pl.ds(0, SENT)], dst_ref=returned.at[mine, pl.ds(0, SENT)],
+                src_ref=result.at[device, pl.ds(0, SENT)], dst_ref=returned.at[mine, pl.ds(0, SENT)],
                 send_sem=return_send.at[0], recv_sem=return_sem.at[0],
-                device_id=(wall, peer), device_id_type=MESH,
+                device_id=(wall, device), device_id_type=MESH,
             ).start()
+
+        for device in EARLY_FIRST:
+            pl.when(me != device)(functools.partial(give_back, device))
         pltpu.make_async_copy(
             result.at[me, pl.ds(0, SENT)], returned.at[mine, pl.ds(0, SENT)], return_sem.at[0]
         ).start()

time: 22.3 us -> 21.7 us (0.973)
  Pallas kernels: 21.4 us -> 20.9 us
    pallas_call x1, Pallas kernels: 19.8 us -> 19.3 us  [on_device(): pl.pallas_call(kernel, out_shape=jax.ShapeDtypeStruct((SOLVERS, ROOM, LAN...]
where the time goes in v8:
time: 21.7 us; the launch traced here: 21.6 us
  Pallas kernels  20.9 us (96%)
  between operations  0.64 us (3%)
    pallas_call x1, Pallas kernels, on_device(): pl.pallas_call(kernel, out_shape=jax.ShapeDtypeStruct((SOLVERS, ROOM, LAN...  19.3 us
    pallas_call x1, Pallas kernels, on_device(): pl.pallas_call(place_rows, out_shape=(jax.ShapeDtypeStruct(pressure.shape...  1.63 us

profile of v8, /device:TPU:1, one launch (start us, length us, event | category | flops | bytes accessed | tf_op | source)
XLA Modules:
  0.0 21.6 jit_solution(9102522455924373758)
XLA Ops:
  0.6 19.3 %shard_map.77.returned = f32[8,24,128]{2,1,0:T(8,128)} custom-call(f32[2,8]{1,0:T(2,128)} %table_in.1, s32[8]{0:T(128)} %contact_in.1, f32[8,16,128]{2,1,0:T(8,128)} %pressure_in.1, s32[8,16,128]{2,1,0:T(8,128)} %layer_in.1, f32[8,16,128]{2,1,0:T(8,128)} %loading_in.1, f32[128]{0:T(128)} %spring_in.1), custom_call_target="tpu_custom_call" | custom-call | tf_op jit(solution)/shard_map/pallas_call | solution.py:524
  19.9 1.6 %shard_map.78 = (f32[8,16,128]{2,1,0:T(8,128)}, f32[128]{0:T(128)}) custom-call(f32[8,24,128]{2,1,0:T(8,128)} %shard_map.77.returned), custom_call_target="tpu_custom_call" | custom-call | tf_op jit(solution)/shard_map/pallas_call | solution.py:559

commit v9 on v8

--- a/solution.py
+++ b/solution.py
@@ -79,17 +79,19 @@
     walls = lax.axis_size("wall")
     has_left, has_right = wall > 0, wall < walls - 1
 
-    def shift_of(wall):
-        return SOLVERS * lax.rem(wall, 2)
-
     def spot_of(device):
-        at = lax.rem(device + BLOCKS - shift_of(wall), BLOCKS)
-        return jnp.where(at < SOLVERS, lax.rem(at + SOLVERS - MOVED, SOLVERS), at)
+        row, at = device // SIDE, device % SIDE
+        place = lax.rem(2 * row + at % 2 + SOLVERS - MOVED, SOLVERS)
+        return jnp.where(at // 2 == lax.rem(wall, 2), place, SOLVERS)
+
+    def device_of(spot, wall):
+        place = (spot + MOVED) % SOLVERS
+        return place // 2 * SIDE + 2 * lax.rem(wall, 2) + place % 2
 
     mine = spot_of(me)
     solves, first, last = mine < SOLVERS, mine == 0, mine == SOLVERS - 1
-    left_end = (wall - 1, shift_of(wall + 1) + (SOLVERS - 1 + MOVED) % SOLVERS)
-    right_end = (wall + 1, shift_of(wall + 1) + MOVED)
+    left_end = (wall - 1, device_of(SOLVERS - 1, wall + 1))
+    right_end = (wall + 1, device_of(0, wall + 1))
 
     inputs = [
         pltpu.make_async_copy(source_ref, here, in_sem.at[at])
@@ -114,19 +116,13 @@
 
     @pl.when(first & has_left)
     def _():
-        def call(k, _):
+        for k in reversed(range(BLOCKS)):
             pl.semaphore_signal(barrier, inc=1, device_id=(wall - 1, k), device_id_type=MESH)
-            return 0
-
-        lax.fori_loop(0, BLOCKS, call, 0)
 
     @pl.when(last & has_right)
     def _():
-        def call(k, _):
+        for k in reversed(range(BLOCKS)):
             pl.semaphore_signal(barrier, inc=1, device_id=(wall + 1, k), device_id_type=MESH)
-            return 0
-
-        lax.fori_loop(0, BLOCKS, call, 0)
 
     def pack(which, ref):
         inputs[which].wait()
@@ -370,10 +366,10 @@
             a2b, a2a = a2 * back_mask, a2 * ahead_mask
             keep[z] = (1.0 - 2.0 * a1 - a2b - a2a) * inverse[z]
             along[z], back[z], ahead[z] = a1 * inverse[z], a2b * inverse[z], a2a * inverse[z]
+        arrived(PRESSURE)
         arrived(LOADING)
         for z in range(ROWS):
             source[z] = source[z] * inverse[z]
-        arrived(PRESSURE)
 
         def solve(_, carry):
             spring_now = springs[...]

time: 21.7 us -> 21.7 us (level)
  no operation moved by 1% of the time
where the time goes in v9:
time: 21.7 us; the launch traced here: 21.5 us
  Pallas kernels  20.9 us (96%)
  between operations  0.64 us (3%)
    pallas_call x1, Pallas kernels, on_device(): pl.pallas_call(kernel, out_shape=jax.ShapeDtypeStruct((SOLVERS, ROOM, LAN...  19.3 us
    pallas_call x1, Pallas kernels, on_device(): pl.pallas_call(place_rows, out_shape=(jax.ShapeDtypeStruct(pressure.shape...  1.63 us

profile of v9, /device:TPU:1, one launch (start us, length us, event | category | flops | bytes accessed | tf_op | source)
XLA Modules:
  0.0 21.5 jit_solution(3150347794724462669)
XLA Ops:
  0.6 19.3 %shard_map.77.returned = f32[8,24,128]{2,1,0:T(8,128)} custom-call(f32[2,8]{1,0:T(2,128)} %table_in.1, s32[8]{0:T(128)} %contact_in.1, f32[8,16,128]{2,1,0:T(8,128)} %pressure_in.1, s32[8,16,128]{2,1,0:T(8,128)} %layer_in.1, f32[8,16,128]{2,1,0:T(8,128)} %loading_in.1, f32[128]{0:T(128)} %spring_in.1), custom_call_target="tpu_custom_call" | custom-call | tf_op jit(solution)/shard_map/pallas_call | solution.py:520
  19.9 1.6 %shard_map.78 = (f32[8,16,128]{2,1,0:T(8,128)}, f32[128]{0:T(128)}) custom-call(f32[8,24,128]{2,1,0:T(8,128)} %shard_map.77.returned), custom_call_target="tpu_custom_call" | custom-call | tf_op jit(solution)/shard_map/pallas_call | solution.py:555

commit v10 on v9

--- a/solution.py
+++ b/solution.py
@@ -169,6 +169,27 @@
     pack(LAYER, layer)
     pack(PRESSURE, pressure)
     pack(LOADING, loading)
+    sides = has_left.astype(jnp.int32) + has_right.astype(jnp.int32)
+    pl.semaphore_wait(barrier, SOLVERS - solves.astype(jnp.int32) + sides)
+
+    @pl.when(has_right)
+    def _():
+        for which in (LAYER, PRESSURE, LOADING):
+            to_right(which).start()
+
+    @pl.when(has_left)
+    def _():
+        for which in (LAYER, PRESSURE, LOADING):
+            to_left(which).start()
+
+    def deal(peer, *arrays):
+        @pl.when(spot_of(peer) < SOLVERS)
+        def _():
+            for which in arrays:
+                to_peer(which, peer).start()
+
+    for peer in peers:
+        deal(peer, LAYER)
     for copy in inputs[LOADING + 1:]:
         copy.wait()
     lane = lax.broadcasted_iota(jnp.int32, (8, LANES), 1)
@@ -187,9 +208,6 @@
         device_id=left_end, device_id_type=MESH,
     )
 
-    sides = has_left.astype(jnp.int32) + has_right.astype(jnp.int32)
-    pl.semaphore_wait(barrier, SOLVERS - solves.astype(jnp.int32) + sides)
-
     @pl.when(first & has_right)
     def _():
         wall_right.start()
@@ -198,24 +216,6 @@
     def _():
         wall_left.start()
 
-    @pl.when(has_right)
-    def _():
-        for which in (LAYER, PRESSURE, LOADING):
-            to_right(which).start()
-
-    @pl.when(has_left)
-    def _():
-        for which in (LAYER, PRESSURE, LOADING):
-            to_left(which).start()
-
-    def deal(peer, *arrays):
-        @pl.when(spot_of(peer) < SOLVERS)
-        def _():
-            for which in arrays:
-                to_peer(which, peer).start()
-
-    for peer in peers:
-        deal(peer, LAYER)
     for peer in peers:
         deal(peer, PRESSURE, LOADING)
 

time: 21.7 us -> 21.7 us (level)
  no operation moved by 1% of the time
where the time goes in v10:
time: 21.7 us; the launch traced here: 21.6 us
  Pallas kernels  20.9 us (96%)
  between operations  0.64 us (3%)
    pallas_call x1, Pallas kernels, on_device(): pl.pallas_call(kernel, out_shape=jax.ShapeDtypeStruct((SOLVERS, ROOM, LAN...  19.3 us
    pallas_call x1, Pallas kernels, on_device(): pl.pallas_call(place_rows, out_shape=(jax.ShapeDtypeStruct(pressure.shape...  1.63 us

profile of v10, /device:TPU:1, one launch (start us, length us, event | category | flops | bytes accessed | tf_op | source)
XLA Modules:
  0.0 21.6 jit_solution(13180943670837656417)
XLA Ops:
  0.6 19.3 %shard_map.77.returned = f32[8,24,128]{2,1,0:T(8,128)} custom-call(f32[2,8]{1,0:T(2,128)} %table_in.1, s32[8]{0:T(128)} %contact_in.1, f32[8,16,128]{2,1,0:T(8,128)} %pressure_in.1, s32[8,16,128]{2,1,0:T(8,128)} %layer_in.1, f32[8,16,128]{2,1,0:T(8,128)} %loading_in.1, f32[128]{0:T(128)} %spring_in.1), custom_call_target="tpu_custom_call" | custom-call | tf_op jit(solution)/shard_map/pallas_call | solution.py:520
  19.9 1.6 %shard_map.78 = (f32[8,16,128]{2,1,0:T(8,128)}, f32[128]{0:T(128)}) custom-call(f32[8,24,128]{2,1,0:T(8,128)} %shard_map.77.returned), custom_call_target="tpu_custom_call" | custom-call | tf_op jit(solution)/shard_map/pallas_call | solution.py:555
